TPU v7x, 128 devices: a whole 4x4x4 slice. The times are simulated.
128 devices in a mesh: section: 2 (over x_hi), dp: 16 (over y, z), seq: 4 (over x_lo, core).
Axes of the slice: x: 4 (x_hi: 2, x_lo: 2; x = x_hi * 2 + x_lo), y: 4, z: 4, core: 2. Of those that a mesh axis runs over, the one named last changes fastest.
Arguments:
- latents: bfloat16 [2, 16, 1024, 768], P(None, 'dp', 'seq'), may hold values from -6 to 6
- conditions: float32 [2, 16, 768], P(None, 'dp'), may hold values from -6 to 6
- output_cotangent: bfloat16 [2, 16, 1024, 768], P(None, 'dp', 'seq'), may hold values from -6 to 6
- modulation_weight: bfloat16 [2, 768, 4608], P('section', 'dp'), may hold values from -0.21875 to 0.21875
- modulation_bias: bfloat16 [2, 4608], P('section', 'dp'), may hold values from -3 to 3
- projection_weight: bfloat16 [2, 768, 2304], P('section', 'dp'), may hold values from -0.21875 to 0.21875
- projection_bias: bfloat16 [2, 1536], P('section', 'dp'), may hold values from -3 to 3
- attention_weight: bfloat16 [2, 768, 768], P('section', 'dp'), may hold values from -1.75 to 1.75
- attention_bias: bfloat16 [2, 768], P('section', 'dp'), may hold values from -2 to 2
- expand_weight: bfloat16 [2, 768, 3072], P('section', 'dp'), may hold values from -0.21875 to 0.21875
- expand_bias: bfloat16 [2, 3072], P('section', 'dp'), may hold values from -3 to 3
- contract_weight: bfloat16 [2, 3072, 768], P('section', 'dp'), may hold values from -0.109375 to 0.109375
- contract_bias: bfloat16 [2, 768], P('section', 'dp'), may hold values from -2 to 2
Outputs:
- section_outputs: bfloat16 [2, 2, 16, 1024, 768], P('section', None, 'dp', 'seq')
- input_grads: float32 [2, 2, 16, 1024, 768], P('section', None, 'dp', 'seq')
- condition_grads: float32 [2, 16, 768], P(None, 'dp')
- modulation_weight_grad: float32 [2, 768, 4608], P('section', 'dp')
- modulation_bias_grad: float32 [2, 4608], P('section', 'dp')
- projection_weight_grad: float32 [2, 768, 2304], P('section', 'dp')
- projection_bias_grad: float32 [2, 1536], P('section', 'dp')
- attention_weight_grad: float32 [2, 768, 768], P('section', 'dp')
- attention_bias_grad: float32 [2, 768], P('section', 'dp')
- expand_weight_grad: float32 [2, 768, 3072], P('section', 'dp')
- expand_bias_grad: float32 [2, 3072], P('section', 'dp')
- contract_weight_grad: float32 [2, 3072, 768], P('section', 'dp')
- contract_bias_grad: float32 [2, 768], P('section', 'dp')
All inputs are finite; a program needn't handle non-finite values.
Results may differ from a plain program's by a relative error of at most 0.02.
The roundings to bfloat16 on the way count: a program that leaves them out, or rounds other values in their place, can miss the bound.
Values may be sent and summed in bfloat16 or wider, within the bound.
A program may use at most 192 MiB of HBM per device.

v0:
```python
import jax
import jax.numpy as jnp
from jax import lax
from jax.sharding import PartitionSpec as P

HEAD = 64


def passed_along(value, axis, steps):
    count = lax.axis_size(axis)
    initial, last = (max(0, -steps), min(count, count - steps))
    return lax.ppermute(value, axis, [(source, source + steps) for source in range(initial, last)])


def norm_rows(values):
    row_mean = jnp.mean(values, axis=-1, keepdims=True)
    centered = values - row_mean
    variance = jnp.mean(centered * centered, axis=-1, keepdims=True)
    inv_std = lax.rsqrt(variance + 1e-06)
    return (centered * inv_std, inv_std)


def norm_back(gradient, normed, inv_std):
    row_mean = jnp.mean(gradient, axis=-1, keepdims=True)
    along = jnp.mean(gradient * normed, axis=-1, keepdims=True)
    return inv_std * (gradient - row_mean - normed * along)


def score_rows(queries, key_rows):
    return jnp.einsum(
        "qhd,khd->hqk", queries, key_rows, preferred_element_type=jnp.float32
    ) * HEAD ** (-0.5)


def attend(queries, key_rows, value_rows):
    scores = score_rows(queries, key_rows)
    row_top = jnp.max(scores, axis=-1, keepdims=True)
    log_total = row_top + jnp.log(jnp.sum(jnp.exp(scores - row_top), axis=-1, keepdims=True))
    weights = jnp.exp(scores - log_total).astype(jnp.bfloat16)
    outputs = jnp.einsum("hqk,khd->qhd", weights, value_rows, preferred_element_type=jnp.float32)
    return (outputs.astype(jnp.bfloat16), log_total[..., 0])


def split_heads(latent_heads):
    length, three, group_width = latent_heads.shape
    split_view = latent_heads.reshape(length, three, group_width // HEAD, HEAD)
    return (split_view[:, 0], split_view[:, 1], split_view[:, 2])


def attend_forward(head_view):
    length = head_view.shape[1]
    group_width = head_view.shape[3]
    block_rows = min(512, length)

    def one_latent(latent_heads):
        queries, key_rows, value_rows = split_heads(latent_heads)
        query_blocks = queries.reshape(length // block_rows, block_rows, queries.shape[1], HEAD)
        outputs, log_totals = lax.map(
            lambda query_block: attend(query_block, key_rows, value_rows), query_blocks
        )
        return (outputs.reshape(length, group_width), log_totals)

    return lax.map(one_latent, head_view)


def attend_backward(head_view, log_totals, head_grads):
    length = head_view.shape[1]
    group_width = head_view.shape[3]
    head_count = group_width // HEAD
    block_rows = min(512, length)
    factor = HEAD ** (-0.5)

    def one_latent(latent_item):
        latent_heads, latent_totals, latent_grads = latent_item
        queries, key_rows, value_rows = split_heads(latent_heads)
        query_blocks = queries.reshape(length // block_rows, block_rows, head_count, HEAD)
        grad_blocks = latent_grads.reshape(length // block_rows, block_rows, head_count, HEAD)

        def block_step(carry, block_item):
            key_sums, value_sums = carry
            query_block, grad_block, total_block = block_item
            probs = jnp.exp(score_rows(query_block, key_rows) - total_block[..., None])
            weights = probs.astype(jnp.bfloat16)
            weight_grads = jnp.einsum(
                "qhd,khd->hqk", grad_block, value_rows, preferred_element_type=jnp.float32
            )
            centre = jnp.sum(probs * weight_grads, axis=-1, keepdims=True)
            score_grads = (probs * (weight_grads - centre)).astype(jnp.bfloat16)
            query_grads = (
                jnp.einsum(
                    "hqk,khd->qhd", score_grads, key_rows, preferred_element_type=jnp.float32
                )
                * factor
            )
            key_sums = (
                key_sums
                + jnp.einsum(
                    "hqk,qhd->khd", score_grads, query_block, preferred_element_type=jnp.float32
                )
                * factor
            )
            value_sums = value_sums + jnp.einsum(
                "hqk,qhd->khd", weights, grad_block, preferred_element_type=jnp.float32
            )
            return ((key_sums, value_sums), query_grads)

        empty = jnp.zeros((length, head_count, HEAD), jnp.float32)
        (key_sums, value_sums), query_grads = lax.scan(
            block_step, (empty, empty), (query_blocks, grad_blocks, latent_totals)
        )
        stacked = jnp.stack(
            [query_grads.reshape(length, head_count, HEAD), key_sums, value_sums], axis=1
        )
        return stacked.astype(jnp.bfloat16).reshape(length, 3, group_width)

    return lax.map(one_latent, (head_view, log_totals, head_grads))


def modulation_pieces(modulation, model_width):
    return [
        modulation[:, None, position * model_width : (position + 1) * model_width]
        for position in range(6)
    ]


def layer_forward(tokens, condition, weights):
    (
        modulation_weight,
        modulation_bias,
        projection_weight,
        projection_bias,
        attention_weight,
        attention_bias,
        expand_weight,
        expand_bias,
        contract_weight,
        contract_bias,
    ) = weights
    latent_count, token_count, model_width = tokens.shape
    silu_cond = jax.nn.silu(condition).astype(jnp.bfloat16)
    modulation = jnp.dot(
        silu_cond, modulation_weight, preferred_element_type=jnp.float32
    ) + modulation_bias.astype(jnp.float32)
    shift_one, scale_one, gate_one, shift_two, scale_two, gate_two = modulation_pieces(
        modulation, model_width
    )
    normed_one, inv_one = norm_rows(tokens.astype(jnp.float32))
    mixed_one = (normed_one * (1.0 + scale_one) + shift_one).astype(jnp.bfloat16)
    full_bias = jnp.concatenate(
        [
            projection_bias[:model_width],
            jnp.zeros((model_width,), jnp.bfloat16),
            projection_bias[model_width:],
        ]
    ).astype(jnp.float32)
    projected = (
        jnp.einsum("ltd,de->lte", mixed_one, projection_weight, preferred_element_type=jnp.float32)
        + full_bias
    )
    projected = projected.astype(jnp.bfloat16).reshape(latent_count, token_count, 3, model_width)
    head_view = lax.all_to_all(projected, "seq", split_axis=3, concat_axis=1, tiled=True)
    attended, log_totals = attend_forward(head_view)
    attended = lax.all_to_all(attended, "seq", split_axis=1, concat_axis=2, tiled=True)
    branch_one = jnp.einsum(
        "ltd,de->lte", attended, attention_weight, preferred_element_type=jnp.float32
    ) + attention_bias.astype(jnp.float32)
    middle = tokens.astype(jnp.float32) + gate_one * branch_one
    normed_two, inv_two = norm_rows(middle)
    mixed_two = (normed_two * (1.0 + scale_two) + shift_two).astype(jnp.bfloat16)
    expanded = jnp.einsum(
        "ltd,df->ltf", mixed_two, expand_weight, preferred_element_type=jnp.float32
    ) + expand_bias.astype(jnp.float32)
    activated = jax.nn.gelu(expanded, approximate=True).astype(jnp.bfloat16)
    branch_two = jnp.einsum(
        "ltf,fd->ltd", activated, contract_weight, preferred_element_type=jnp.float32
    ) + contract_bias.astype(jnp.float32)
    result = (middle + gate_two * branch_two).astype(jnp.bfloat16)
    kept_state = (
        silu_cond,
        modulation,
        normed_one,
        inv_one,
        mixed_one,
        head_view,
        log_totals,
        attended,
        branch_one,
        normed_two,
        inv_two,
        mixed_two,
        expanded,
        activated,
        branch_two,
    )
    return (result, kept_state)


def layer_backward(kept_state, gradient, condition, weights, grad_sums, active):
    (
        modulation_weight,
        modulation_bias,
        projection_weight,
        projection_bias,
        attention_weight,
        attention_bias,
        expand_weight,
        expand_bias,
        contract_weight,
        contract_bias,
    ) = weights
    (
        silu_cond,
        modulation,
        normed_one,
        inv_one,
        mixed_one,
        head_view,
        log_totals,
        attended,
        branch_one,
        normed_two,
        inv_two,
        mixed_two,
        expanded,
        activated,
        branch_two,
    ) = kept_state
    latent_count, token_count, model_width = gradient.shape
    shift_one, scale_one, gate_one, shift_two, scale_two, gate_two = modulation_pieces(
        modulation, model_width
    )
    branch_two_grad = (gate_two * gradient).astype(jnp.bfloat16)
    gate_two_grad = jnp.sum(gradient * branch_two, axis=1)
    contract_weight_grad = jnp.einsum(
        "ltf,ltd->fd", activated, branch_two_grad, preferred_element_type=jnp.float32
    )
    contract_bias_grad = jnp.sum(branch_two_grad.astype(jnp.float32), axis=(0, 1))
    activated_grad = jnp.einsum(
        "ltd,fd->ltf", branch_two_grad, contract_weight, preferred_element_type=jnp.float32
    )
    gelu_pull = jax.vjp(lambda inner: jax.nn.gelu(inner, approximate=True), expanded)[1]
    expanded_grad = gelu_pull(activated_grad)[0].astype(jnp.bfloat16)
    expand_weight_grad = jnp.einsum(
        "ltd,ltf->df", mixed_two, expanded_grad, preferred_element_type=jnp.float32
    )
    expand_bias_grad = jnp.sum(expanded_grad.astype(jnp.float32), axis=(0, 1))
    mixed_two_grad = jnp.einsum(
        "ltf,df->ltd", expanded_grad, expand_weight, preferred_element_type=jnp.float32
    )
    scale_two_grad = jnp.sum(mixed_two_grad * normed_two, axis=1)
    shift_two_grad = jnp.sum(mixed_two_grad, axis=1)
    middle_grad = gradient + norm_back(mixed_two_grad * (1.0 + scale_two), normed_two, inv_two)
    branch_one_grad = (gate_one * middle_grad).astype(jnp.bfloat16)
    gate_one_grad = jnp.sum(middle_grad * branch_one, axis=1)
    attention_weight_grad = jnp.einsum(
        "ltd,lte->de", attended, branch_one_grad, preferred_element_type=jnp.float32
    )
    attention_bias_grad = jnp.sum(branch_one_grad.astype(jnp.float32), axis=(0, 1))
    attended_grad = jnp.einsum(
        "lte,de->ltd", branch_one_grad, attention_weight, preferred_element_type=jnp.float32
    ).astype(jnp.bfloat16)
    head_grads = lax.all_to_all(attended_grad, "seq", split_axis=2, concat_axis=1, tiled=True)
    projected_grad = attend_backward(head_view, log_totals, head_grads)
    projected_grad = lax.all_to_all(projected_grad, "seq", split_axis=1, concat_axis=3, tiled=True)
    projected_grad = projected_grad.reshape(latent_count, token_count, 3 * model_width)
    projection_weight_grad = jnp.einsum(
        "ltd,lte->de", mixed_one, projected_grad, preferred_element_type=jnp.float32
    )
    column_sums = jnp.sum(projected_grad.astype(jnp.float32), axis=(0, 1))
    projection_bias_grad = jnp.concatenate(
        [column_sums[:model_width], column_sums[2 * model_width :]]
    )
    mixed_one_grad = jnp.einsum(
        "lte,de->ltd", projected_grad, projection_weight, preferred_element_type=jnp.float32
    )
    scale_one_grad = jnp.sum(mixed_one_grad * normed_one, axis=1)
    shift_one_grad = jnp.sum(mixed_one_grad, axis=1)
    input_grad = middle_grad + norm_back(mixed_one_grad * (1.0 + scale_one), normed_one, inv_one)
    local_terms = jnp.concatenate(
        [
            shift_one_grad,
            scale_one_grad,
            gate_one_grad,
            shift_two_grad,
            scale_two_grad,
            gate_two_grad,
        ],
        axis=-1,
    )
    modulation_grad = lax.psum(local_terms, "seq").astype(jnp.bfloat16)
    owner = (lax.axis_index("seq") == 0).astype(jnp.float32)
    modulation_weight_grad = (
        jnp.einsum("ld,le->de", silu_cond, modulation_grad, preferred_element_type=jnp.float32)
        * owner
    )
    modulation_bias_grad = jnp.sum(modulation_grad.astype(jnp.float32), axis=0) * owner
    cond_term = jnp.einsum(
        "le,de->ld", modulation_grad, modulation_weight, preferred_element_type=jnp.float32
    )
    silu_pull = jax.vjp(jax.nn.silu, condition)[1]
    condition_grad = silu_pull(cond_term)[0]
    fresh = (
        modulation_weight_grad,
        modulation_bias_grad,
        projection_weight_grad,
        projection_bias_grad,
        attention_weight_grad,
        attention_bias_grad,
        expand_weight_grad,
        expand_bias_grad,
        contract_weight_grad,
        contract_bias_grad,
    )
    grad_sums = tuple((running + active * added for running, added in zip(grad_sums, fresh)))
    return (input_grad, condition_grad, grad_sums)


def on_device(
    latents,
    conditions,
    output_cotangent,
    modulation_weight,
    modulation_bias,
    projection_weight,
    projection_bias,
    attention_weight,
    attention_bias,
    expand_weight,
    expand_bias,
    contract_weight,
    contract_bias,
):
    is_first = lax.axis_index("section") == 0
    first_flag = is_first.astype(jnp.float32)
    later_flag = 1.0 - first_flag
    gathered = (
        lax.all_gather(modulation_weight[0], "dp", axis=0, tiled=True),
        lax.all_gather(modulation_bias[0], "dp", axis=0, tiled=True),
        lax.all_gather(projection_weight[0], "dp", axis=0, tiled=True),
        lax.all_gather(projection_bias[0], "dp", axis=0, tiled=True),
        lax.all_gather(attention_weight[0], "dp", axis=0, tiled=True),
        lax.all_gather(attention_bias[0], "dp", axis=0, tiled=True),
        lax.all_gather(expand_weight[0], "dp", axis=0, tiled=True),
        lax.all_gather(expand_bias[0], "dp", axis=0, tiled=True),
        lax.all_gather(contract_weight[0], "dp", axis=0, tiled=True),
        lax.all_gather(contract_bias[0], "dp", axis=0, tiled=True),
    )

    def send_ahead(values):
        return passed_along(values, "section", 1)

    def send_back(values):
        return passed_along(values, "section", -1)

    lead_output, lead_state = layer_forward(latents[0], conditions[0], gathered)
    arrived = send_ahead(lead_output)
    middle_input = jnp.where(is_first, latents[1], arrived)
    middle_cond = jnp.where(is_first, conditions[1], conditions[0])
    middle_output, middle_state = layer_forward(middle_input, middle_cond, gathered)
    arrived_late = send_ahead(middle_output)
    grad_sums = tuple((jnp.zeros(values.shape, jnp.float32) for values in gathered))
    tail_output, tail_state = layer_forward(arrived_late, conditions[1], gathered)
    tail_grad, tail_cond, grad_sums = layer_backward(
        tail_state,
        output_cotangent[1].astype(jnp.float32),
        conditions[1],
        gathered,
        grad_sums,
        later_flag,
    )
    returned = send_back(tail_grad.astype(jnp.bfloat16))
    middle_grad_in = jnp.where(
        is_first, returned.astype(jnp.float32), output_cotangent[0].astype(jnp.float32)
    )
    middle_grad, middle_cond_grad, grad_sums = layer_backward(
        middle_state, middle_grad_in, middle_cond, gathered, grad_sums, 1.0
    )
    returned_late = send_back(middle_grad.astype(jnp.bfloat16))
    lead_grad, lead_cond, grad_sums = layer_backward(
        lead_state,
        returned_late.astype(jnp.float32),
        conditions[0],
        gathered,
        grad_sums,
        first_flag,
    )
    first_out = jnp.where(is_first, lead_output, middle_output)
    second_out = jnp.where(is_first, middle_output, tail_output)
    section_outputs = jnp.stack([first_out, second_out])[None]
    rounded_middle = middle_grad.astype(jnp.bfloat16).astype(jnp.float32)
    rounded_tail = tail_grad.astype(jnp.bfloat16).astype(jnp.float32)
    first_grad = jnp.where(is_first, lead_grad, rounded_middle)
    second_grad = jnp.where(is_first, middle_grad, rounded_tail)
    input_grads = jnp.stack([first_grad, second_grad])[None]
    cond_terms = jnp.stack(
        [
            jnp.where(is_first, lead_cond, middle_cond_grad),
            jnp.where(is_first, middle_cond_grad, tail_cond),
        ]
    )
    condition_grads = lax.psum(cond_terms, "section")
    owned = (
        lax.psum_scatter(
            grad_sums[0].astype(jnp.bfloat16), "dp", scatter_dimension=0, tiled=True
        ).astype(jnp.float32),
        lax.psum_scatter(
            grad_sums[1].astype(jnp.bfloat16), "dp", scatter_dimension=0, tiled=True
        ).astype(jnp.float32),
        lax.psum_scatter(
            grad_sums[2].astype(jnp.bfloat16), "dp", scatter_dimension=0, tiled=True
        ).astype(jnp.float32),
        lax.psum_scatter(
            grad_sums[3].astype(jnp.bfloat16), "dp", scatter_dimension=0, tiled=True
        ).astype(jnp.float32),
        lax.psum_scatter(
            grad_sums[4].astype(jnp.bfloat16), "dp", scatter_dimension=0, tiled=True
        ).astype(jnp.float32),
        lax.psum_scatter(
            grad_sums[5].astype(jnp.bfloat16), "dp", scatter_dimension=0, tiled=True
        ).astype(jnp.float32),
        lax.psum_scatter(
            grad_sums[6].astype(jnp.bfloat16), "dp", scatter_dimension=0, tiled=True
        ).astype(jnp.float32),
        lax.psum_scatter(
            grad_sums[7].astype(jnp.bfloat16), "dp", scatter_dimension=0, tiled=True
        ).astype(jnp.float32),
        lax.psum_scatter(
            grad_sums[8].astype(jnp.bfloat16), "dp", scatter_dimension=0, tiled=True
        ).astype(jnp.float32),
        lax.psum_scatter(
            grad_sums[9].astype(jnp.bfloat16), "dp", scatter_dimension=0, tiled=True
        ).astype(jnp.float32),
    )
    reduced = (
        lax.psum(owned[0].astype(jnp.bfloat16), "seq").astype(jnp.float32),
        lax.psum(owned[1].astype(jnp.bfloat16), "seq").astype(jnp.float32),
        lax.psum(owned[2].astype(jnp.bfloat16), "seq").astype(jnp.float32),
        lax.psum(owned[3].astype(jnp.bfloat16), "seq").astype(jnp.float32),
        lax.psum(owned[4].astype(jnp.bfloat16), "seq").astype(jnp.float32),
        lax.psum(owned[5].astype(jnp.bfloat16), "seq").astype(jnp.float32),
        lax.psum(owned[6].astype(jnp.bfloat16), "seq").astype(jnp.float32),
        lax.psum(owned[7].astype(jnp.bfloat16), "seq").astype(jnp.float32),
        lax.psum(owned[8].astype(jnp.bfloat16), "seq").astype(jnp.float32),
        lax.psum(owned[9].astype(jnp.bfloat16), "seq").astype(jnp.float32),
    )
    return (
        section_outputs,
        input_grads,
        condition_grads,
        reduced[0][None],
        reduced[1][None],
        reduced[2][None],
        reduced[3][None],
        reduced[4][None],
        reduced[5][None],
        reduced[6][None],
        reduced[7][None],
        reduced[8][None],
        reduced[9][None],
    )


def solution(mesh):
    return jax.shard_map(
        on_device,
        mesh=mesh,
        in_specs=(
            P(None, "dp", "seq", None),
            P(None, "dp", None),
            P(None, "dp", "seq", None),
            P("section", "dp", None),
            P("section", "dp"),
            P("section", "dp", None),
            P("section", "dp"),
            P("section", "dp", None),
            P("section", "dp"),
            P("section", "dp", None),
            P("section", "dp"),
            P("section", "dp", None),
            P("section", "dp"),
        ),
        out_specs=(
            P("section", None, "dp", "seq", None),
            P("section", None, "dp", "seq", None),
            P(None, "dp", None),
            P("section", "dp", None),
            P("section", "dp"),
            P("section", "dp", None),
            P("section", "dp"),
            P("section", "dp", None),
            P("section", "dp"),
            P("section", "dp", None),
            P("section", "dp"),
            P("section", "dp", None),
            P("section", "dp"),
        ),
        check_vma=False,
    )
```

profile of v0, /device:TPU:1, one launch (start us, length us, event | category | flops | bytes accessed | tf_op | source)
XLA Modules:
  0.0 1198.6 jit_solution(14377423073008772429)
XLA Ops:
  18.9 63.4 %all-reduce.12 = (bf16[1536]{0:T(1024)(128)(2,1)S(1)}, bf16[4608]{0:T(1024)(128)(2,1)S(1)}, bf16[768]{0:T(1024)(128)(2,1)}, bf16[768]{0:T(1024)(128)(2,1)}, bf16[3072]{0:T(1024)(128)(2,1)}) all-reduce(bf16[1536]{0:T(1024)(128)(2,1)S(1)} %dynamic-update-slice.1, ...), channel_id=5, replica_groups=mesh['section'=2,'dp'=16,'seq'=4] {'dp'}, use_global_device_ids=true, to_apply=%add.1 | all-reduce | flops 10752 | bytes 43008
  95.3 34.6 %all-gather.18.cloned.1.call-done = bf16[1,768,2304]{2,1,0:T(8,128)(2,1)} async-done(((bf16[1,48,2304]{2,1,0:T(8,128)(2,1)}), bf16[1,768,2304]{2,1,0:T(8,128)(2,1)}) %all-gather.18.cloned.1.call-update) | async-done | bytes 3538960 | tf_op jit(solution)/shard_map/all_gather | solution.py:339
  140.7 19.2 %all-to-all-done = bf16[1,256,3,768]{1,2,0,3:T(4,128)(2,1)S(1)} async-done(((bf16[1,256,3,768]{1,2,0,3:T(4,128)(2,1)}), bf16[1,256,3,768]{1,2,0,3:T(4,128)(2,1)S(1)}, u32[]{:S(2)}, u32[]{:S(2)}) %all-to-all-start) | async-done | bytes 1179680 | tf_op jit(solution)/shard_map/all_to_all | solution.py:161
  162.3 7.5 while.135
  193.8 36.2 %all-gather.22.cloned.1.call-done = bf16[1,768,3072]{2,1,0:T(8,128)(2,1)} async-done(((bf16[1,48,3072]{2,1,0:T(8,128)(2,1)}), bf16[1,768,3072]{2,1,0:T(8,128)(2,1)}) %all-gather.22.cloned.1.call-update) | async-done | bytes 4718608 | tf_op jit(solution)/shard_map/all_gather | solution.py:343
  235.6 50.2 %all-gather.24.cloned.1.call-done = bf16[1,3072,768]{2,1,0:T(8,128)(2,1)} async-done(((bf16[1,192,768]{2,1,0:T(8,128)(2,1)}), bf16[1,3072,768]{2,1,0:T(8,128)(2,1)}) %all-gather.24.cloned.1.call-update) | async-done | bytes 4718608 | tf_op jit(solution)/shard_map/all_gather | solution.py:345
  296.8 7.1 collective-permute-done
  314.0 19.2 %all-to-all-done.2 = bf16[1,256,3,768]{1,2,0,3:T(4,128)(2,1)S(1)} async-done(((bf16[1,256,3,768]{1,2,0,3:T(4,128)(2,1)}), bf16[1,256,3,768]{1,2,0,3:T(4,128)(2,1)S(1)}, u32[]{:S(2)}, u32[]{:S(2)}) %all-to-all-start.2) | async-done | bytes 1179680 | tf_op jit(solution)/shard_map/all_to_all | solution.py:161
  335.6 7.5 while.136
  351.3 10.5 all_to_all.180
  380.5 6.6 collective-permute-done.1
  402.1 19.3 %all-to-all-done.4 = bf16[1,256,3,768]{1,2,0,3:T(4,128)(2,1)} async-done(((bf16[1,256,3,768]{1,2,0,3:T(4,128)(2,1)}), bf16[1,256,3,768]{1,2,0,3:T(4,128)(2,1)}, u32[]{:S(2)}, u32[]{:S(2)}) %all-to-all-start.4) | async-done | bytes 1179680 | tf_op jit(solution)/shard_map/all_to_all | solution.py:161
  430.0 7.5 while.137
  447.0 11.1 all_to_all.181
  488.3 6.5 all-to-all-done.6
  496.8 27.2 %while.138 = (s32[]{:T(128)}, f32[1024,3,64]{0,2,1:T(8,128)}, f32[1024,3,64]{0,2,1:T(8,128)}, bf16[2,512,3,64]{1,3,2,0:T(8,128)(2,1)}, bf16[2,512,3,64]{1,3,2,0:...) while((s32[]{:T(128)}, f32[1024,3,64]{0,2,1:T(8,128)}, ...), condition=%wide.region_28.29_spmd.clone, body=%wide.region_26.28_spmd.clone.sunk | while | flops 1026587136 | bytes 112506744 | solution.py:108
  529.6 28.8 %all_to_all.182 = bf16[1,1024,3,192]{3,2,0,1:T(4,128)(2,1)} all-to-all(bf16[1,1024,3,192]{3,2,0,1:T(4,128)(2,1)S(1)} %copy.277), channel_id=1, replica_groups=mesh['section'=2,'dp'=16,'seq'=4] {'seq'}, dimensions={1} | all-to-all | bytes 2359296 | tf_op jit(solution)/shard_map/all_to_all | solution.py:264
  570.4 11.7 collective-permute-done.2
  613.6 29.1 %while.139 = (s32[]{:T(128)}, f32[1024,3,64]{0,2,1:T(8,128)}, f32[1024,3,64]{0,2,1:T(8,128)}, bf16[2,512,3,64]{1,3,2,0:T(8,128)(2,1)}, bf16[2,512,3,64]{1,3,2,0:...) while((s32[]{:T(128)}, f32[1024,3,64]{0,2,1:T(8,128)}, ...), condition=%wide.region_35.36_spmd.clone, body=%wide.region_33.35_spmd.clone.sunk | while | flops 1026587136 | bytes 107788576 | solution.py:108
  654.0 24.8 %all-to-all-done.9 = bf16[1,1024,3,192]{3,2,0,1:T(4,128)(2,1)S(1)} async-done(((bf16[1,1024,3,192]{3,2,0,1:T(4,128)(2,1)}), bf16[1,1024,3,192]{3,2,0,1:T(4,128)(2,1)S(1)}, u32[]{:S(2)}, u32[]{:S(2)}) %all-to-all-start.9) | async-done | bytes 1179680 | tf_op jit(solution)/shard_map/all_to_all | solution.py:264
  696.0 8.9 collective-permute-done.3
  735.9 29.3 %while.140 = (s32[]{:T(128)}, f32[1024,3,64]{0,2,1:T(8,128)}, f32[1024,3,64]{0,2,1:T(8,128)}, bf16[2,512,3,64]{1,3,2,0:T(8,128)(2,1)}, bf16[2,512,3,64]{1,3,2,0:...) while((s32[]{:T(128)}, f32[1024,3,64]{0,2,1:T(8,128)}, ...), condition=%wide.region_42.43_spmd.clone, body=%wide.region_40.42_spmd.clone.sunk | while | flops 1026587136 | bytes 107788576 | solution.py:108
  786.7 14.8 %all-to-all-done.11 = bf16[1,1024,3,192]{3,2,0,1:T(4,128)(2,1)S(1)} async-done(((bf16[1,1024,3,192]{3,2,0,1:T(4,128)(2,1)}), bf16[1,1024,3,192]{3,2,0,1:T(4,128)(2,1)S(1)}, u32[]{:S(2)}, u32[]{:S(2)}) %all-to-all-start.11) | async-done | bytes 1179680 | tf_op jit(solution)/shard_map/all_to_all | solution.py:264
  805.6 8.5 add_convert_fusion.3
  825.4 7.0 add_convert_fusion.1
  853.7 14.8 %all-reduce.10 = (bf16[1,4608]{1,0:T(2,128)(2,1)S(1)}, bf16[1,4608]{1,0:T(2,128)(2,1)S(1)}, bf16[1,4608]{1,0:T(2,128)(2,1)S(1)}) all-reduce(f32[1,4608]{1,0:T(1,128)S(1)} %constant_dynamic-update-slice_fusion.12, f32[1,4608]{1,0:T(1,128)S(1)} %constant_dynamic-update-slice_fusion.6, ...), channel_id=1, replica_groups=mesh['section'=2,'dp'=16,'seq'=4] {'seq'}, use_global_device_ids=true, to_apply=%region_65.66 | all-reduce | flops 13824 | bytes 82944 | tf_op jit(solution)/shard_map/psum | solution.py:290
  868.8 7.0 add_convert_fusion
  886.9 58.9 %all-reduce.11 = (bf16[4608]{0:T(1024)(128)(2,1)S(1)}, bf16[1536]{0:T(1024)(128)(2,1)S(1)}, bf16[768]{0:T(1024)(128)(2,1)S(1)}, bf16[3072]{0:T(1024)(128)(2,1)S(1)}, bf16[768]{0:T(1024)(128)(2,1)S(1)}) all-reduce(bf16[4608]{0:T(1024)(128)(2,1)S(1)} %get-tuple-element.834, ...), channel_id=13, replica_groups=mesh['section'=2,'dp'=16,'seq'=4] {'dp'}, use_global_device_ids=true, to_apply=%region_69.70.clone | all-reduce | flops 10752 | bytes 43008
  946.2 20.6 %all-reduce.13 = (bf16[1,288]{1,0:T(2,128)(2,1)S(1)}, bf16[1,96]{1,0:T(2,128)(2,1)S(1)}, bf16[1,48]{1,0:T(2,128)(2,1)S(1)}, bf16[1,192]{1,0:T(2,128)(2,1)S(1)}, bf16[1,48]{1,0:T(2,128)(2,1)S(1)}) all-reduce(bf16[1,288]{1,0:T(2,128)(2,1)S(1)} %broadcast_in_dim.205, ...), channel_id=1, replica_groups=mesh['section'=2,'dp'=16,'seq'=4] {'seq'}, use_global_device_ids=true, to_apply=%region_70.71 | all-reduce | flops 672 | bytes 2688 | tf_op jit(solution)/shard_map/psum | solution.py:436
  974.5 74.3 %reduce-scatter.12.cloned.1.call-done = bf16[48,3072]{1,0:T(8,128)(2,1)} async-done(((bf16[768,3072]{1,0:T(8,128)(2,1)}), bf16[48,3072]{1,0:T(8,128)(2,1)}) %reduce-scatter.12.cloned.1.call-update) | async-done | bytes 294928 | tf_op jit(solution)/shard_map/reduce_scatter | solution.py:421
  1048.8 85.8 %reduce-scatter.6.cloned.1.call-done = bf16[48,4608]{1,0:T(8,128)(2,1)} async-done(((bf16[768,4608]{1,0:T(8,128)(2,1)}), bf16[48,4608]{1,0:T(8,128)(2,1)}) %reduce-scatter.6.cloned.1.call-update) | async-done | bytes 442384 | tf_op jit(solution)/shard_map/reduce_scatter | solution.py:403
  1152.0 32.4 %all-reduce.17.cloned.1.call-done = (bf16[1,48,4608]{2,1,0:T(8,128)(2,1)}, bf16[1,48,2304]{2,1,0:T(8,128)(2,1)}, bf16[1,48,768]{2,1,0:T(8,128)(2,1)}, bf16[1,48,3072]{2,1,0:T(8,128)(2,1)}, bf16[1,192,768]{2,1,0:T(8,128)(2,1)}) async-done(((bf16[1,48,4608]{2,1,0:T(8,128)(2,1)}, bf16[1,48,2304]{2,1,0:T(8,128)(2,1)}, bf16[1,48,768]{2,1,0:T(8,128)(2,1)}, bf16[1,48,3072]{2,1,0:T(8,128)(2,1)}, ...) | async-done | bytes 1327120 | tf_op jit(solution)/shard_map/psum | solution.py:435
  (944 shorter events, 492.7 us)
Async XLA Ops:
  7.2 79.6 %all-gather.16.cloned.1.call-start = ((), (), s32[]{:S(2)}) async-start(), calls=%async_computation.22 | async-start | bytes 7520256 | tf_op jit(solution)/shard_map/all_gather | solution.py:337
  7.9 122.0 %all-gather.18.cloned.1.call-start = ((), (), s32[]{:S(2)}) async-start(), calls=%async_computation.23 | async-start | bytes 3760128 | tf_op jit(solution)/shard_map/all_gather | solution.py:339
  8.7 182.1 %all-gather.20.cloned.1.call-start = ((), (), s32[]{:S(2)}) async-start(), calls=%async_computation.24 | async-start | bytes 1253376 | tf_op jit(solution)/shard_map/all_gather | solution.py:341
  9.4 220.6 %all-gather.22.cloned.1.call-start = ((), (), s32[]{:S(2)}) async-start(), calls=%async_computation.25 | async-start | bytes 5013504 | tf_op jit(solution)/shard_map/all_gather | solution.py:343
  10.0 275.8 %all-gather.24.cloned.1.call-start = ((), (), s32[]{:S(2)}) async-start(), calls=%async_computation.26 | async-start | bytes 5013504 | tf_op jit(solution)/shard_map/all_gather | solution.py:345
  95.3 134.7 %copy-start.147 = (f32[768]{0:T(1024)}, f32[768]{0:T(1024)S(1)}, u32[]{:S(2)}) copy-start(f32[768]{0:T(1024)S(1)} %get-tuple-element.852) | copy-start | bytes 9220
  95.3 195.7 %copy-start.140 = (f32[768]{0:T(1024)}, f32[768]{0:T(1024)S(1)}, u32[]{:S(2)}) copy-start(f32[768]{0:T(1024)S(1)} %get-tuple-element.850) | copy-start | bytes 9220
  135.9 24.0 %all-to-all-start = ((bf16[1,256,3,768]{1,2,0,3:T(4,128)(2,1)}), bf16[1,256,3,768]{1,2,0,3:T(4,128)(2,1)S(1)}, u32[]{:S(2)}, u32[]{:S(2)}) async-start(bf16[1,256,3,768]{1,2,0,3:T(4,128)(2,1)} %copy.246), calls=%async_computation | async-start | bytes 3145728 | tf_op jit(solution)/shard_map/all_to_all | solution.py:161
  177.9 11.1 all-to-all-start.1
  183.2 182.1 %copy-start.144 = (f32[768]{0:T(1024)}, f32[768]{0:T(1024)S(1)}, u32[]{:S(2)}) copy-start(f32[768]{0:T(1024)S(1)} %convert_element_type.597) | copy-start | bytes 9220
  184.5 101.3 %copy-start.230 = (f32[768]{0:T(1024)}, f32[768]{0:T(1024)S(1)}, u32[]{:S(2)}) copy-start(f32[768]{0:T(1024)S(1)} %convert_element_type.599) | copy-start | bytes 9220
  193.6 97.5 %copy-start.26 = (f32[256,768]{1,0:T(8,128)}, f32[256,768]{1,0:T(8,128)S(1)}, u32[]{:S(2)}) copy-start(f32[256,768]{1,0:T(8,128)S(1)} %get-tuple-element.1004) | copy-start | bytes 2359300
  291.2 12.6 %collective-permute-start = (bf16[1,256,768]{2,1,0:T(8,128)(2,1)S(1)}, bf16[1,256,768]{2,1,0:T(8,128)(2,1)S(1)}, u32[]{:S(2)}, u32[]{:S(2)}) collective-permute-start(bf16[1,256,768]{2,1,0:T(8,128)(2,1)S(1)} %fusion.312), channel_id=1, source_target_pairs={{0,64},{1,65},{2,66},{3,67},{4,68},{5,69},{6,70},{7,71},{8,72},{9,... | collective-permute-start | bytes 1179656 | tf_op jit(solution)/shard_map/ppermute | solution.py:12
  308.4 24.7 %all-to-all-start.2 = ((bf16[1,256,3,768]{1,2,0,3:T(4,128)(2,1)}), bf16[1,256,3,768]{1,2,0,3:T(4,128)(2,1)S(1)}, u32[]{:S(2)}, u32[]{:S(2)}) async-start(bf16[1,256,3,768]{1,2,0,3:T(4,128)(2,1)} %copy.255), calls=%async_computation.2 | async-start | bytes 3145728 | tf_op jit(solution)/shard_map/all_to_all | solution.py:161
  374.1 13.1 %collective-permute-start.1 = (bf16[1,256,768]{2,1,0:T(8,128)(2,1)S(1)}, bf16[1,256,768]{2,1,0:T(8,128)(2,1)S(1)}, u32[]{:S(2)}, u32[]{:S(2)}) collective-permute-start(bf16[1,256,768]{2,1,0:T(8,128)(2,1)S(1)} %get-tuple-element.996), channel_id=1, source_target_pairs={{0,64},{1,65},{2,66},{3,67},{4,68},{5,69},{6,70},{7,71},{8,72},{9,... | collective-permute-start | bytes 1179656 | tf_op jit(solution)/shard_map/ppermute | solution.py:12
  380.5 187.4 %copy-start.115 = (f32[768]{0:T(1024)}, f32[768]{0:T(1024)S(1)}, u32[]{:S(2)}) copy-start(f32[768]{0:T(1024)S(1)} %get-tuple-element.842) | copy-start | bytes 9220
  380.5 211.3 %copy-start.142 = (f32[768]{0:T(1024)}, f32[768]{0:T(1024)S(1)}, u32[]{:S(2)}) copy-start(f32[768]{0:T(1024)S(1)} %get-tuple-element.838) | copy-start | bytes 9220
  395.6 25.8 %all-to-all-start.4 = ((bf16[1,256,3,768]{1,2,0,3:T(4,128)(2,1)}), bf16[1,256,3,768]{1,2,0,3:T(4,128)(2,1)}, u32[]{:S(2)}, u32[]{:S(2)}) async-start(bf16[1,256,3,768]{1,2,0,3:T(4,128)(2,1)} %copy.264), calls=%async_computation.4 | async-start | bytes 3145728 | tf_op jit(solution)/shard_map/all_to_all | solution.py:161
  483.7 11.2 all-to-all-start.6
  568.9 13.2 %collective-permute-start.2 = (bf16[1,256,768]{2,1,0:T(8,128)(2,1)S(1)}, bf16[1,256,768]{2,1,0:T(8,128)(2,1)S(1)}, u32[]{:S(2)}, u32[]{:S(2)}) collective-permute-start(bf16[1,256,768]{2,1,0:T(8,128)(2,1)S(1)} %get-tuple-element.1033), channel_id=1, source_target_pairs={{64,0},{65,1},{66,2},{67,3},{68,4},{69,5},{70,6},{71,7},{72,8},{73... | collective-permute-start | bytes 1179656 | tf_op jit(solution)/shard_map/ppermute | solution.py:12
  599.6 12.2 %all-to-all-start.8 = ((bf16[4,2,24576]{2,1,0:T(2,128)(2,1)}), bf16[4,2,24576]{2,1,0:T(2,128)(2,1)S(1)}, u32[]{:S(2)}, u32[]{:S(2)}) async-start(bf16[4,2,24576]{2,1,0:T(2,128)(2,1)} %reshape.1500), calls=%async_computation.8 | async-start | bytes 786432 | tf_op jit(solution)/shard_map/all_to_all | solution.py:262
  649.5 29.3 %all-to-all-start.9 = ((bf16[1,1024,3,192]{3,2,0,1:T(4,128)(2,1)}), bf16[1,1024,3,192]{3,2,0,1:T(4,128)(2,1)S(1)}, u32[]{:S(2)}, u32[]{:S(2)}) async-start(bf16[1,1024,3,192]{3,2,0,1:T(4,128)(2,1)} %copy.285), calls=%async_computation.9 | async-start | bytes 4194304 | tf_op jit(solution)/shard_map/all_to_all | solution.py:264
  691.5 13.4 %collective-permute-start.3 = (bf16[1,256,768]{2,1,0:T(8,128)(2,1)S(1)}, bf16[1,256,768]{2,1,0:T(8,128)(2,1)S(1)}, u32[]{:S(2)}, u32[]{:S(2)}) collective-permute-start(bf16[1,256,768]{2,1,0:T(8,128)(2,1)S(1)} %get-tuple-element.993), channel_id=1, source_target_pairs={{64,0},{65,1},{66,2},{67,3},{68,4},{69,5},{70,6},{71,7},{72,8},{73... | collective-permute-start | bytes 1179656 | tf_op jit(solution)/shard_map/ppermute | solution.py:12
  722.2 11.8 all-to-all-start.10
  727.4 247.0 %reduce-scatter.10.cloned.1.call-start = ((), (), s32[]{:S(2)}) async-start(), calls=%async_computation.19 | async-start | bytes 1253376 | tf_op jit(solution)/shard_map/reduce_scatter | solution.py:415
  772.1 29.4 %all-to-all-start.11 = ((bf16[1,1024,3,192]{3,2,0,1:T(4,128)(2,1)}), bf16[1,1024,3,192]{3,2,0,1:T(4,128)(2,1)S(1)}, u32[]{:S(2)}, u32[]{:S(2)}) async-start(bf16[1,1024,3,192]{3,2,0,1:T(4,128)(2,1)} %copy.293), calls=%async_computation.11 | async-start | bytes 4194304 | tf_op jit(solution)/shard_map/all_to_all | solution.py:264
  776.6 197.9 %reduce-scatter.8.cloned.1.call-start = ((), (), s32[]{:S(2)}) async-start(), calls=%async_computation.18 | async-start | bytes 3760128 | tf_op jit(solution)/shard_map/reduce_scatter | solution.py:409
  814.1 160.3 %reduce-scatter.14.cloned.1.call-start = ((), (), s32[]{:S(2)}) async-start(), calls=%async_computation.21 | async-start | bytes 5013504 | tf_op jit(solution)/shard_map/reduce_scatter | solution.py:427
  832.5 216.3 %reduce-scatter.12.cloned.1.call-start = ((), (), s32[]{:S(2)}) async-start(), calls=%async_computation.20 | async-start | bytes 5013504 | tf_op jit(solution)/shard_map/reduce_scatter | solution.py:421
  842.9 291.7 %reduce-scatter.6.cloned.1.call-start = ((), (), s32[]{:S(2)}) async-start(), calls=%async_computation.17 | async-start | bytes 7520256 | tf_op jit(solution)/shard_map/reduce_scatter | solution.py:403
  875.9 308.6 %all-reduce.17.cloned.1.call-start = ((), (), s32[]{:S(2)}) async-start(), calls=%async_computation.27 | async-start | bytes 2654208 | tf_op jit(solution)/shard_map/psum | solution.py:435
  969.4 165.2 %copy-start.136 = (bf16[1,4608]{1,0:T(2,128)(2,1)S(1)}, bf16[1,4608]{1,0:T(2,128)(2,1)}, u32[]{:S(2)}) copy-start(bf16[1,4608]{1,0:T(2,128)(2,1)} %copy-done.135) | copy-start | bytes 27652
  (256 other events, 2728.7 us)
Sparse Core Ops, SparseCore 0:
  10.2 68.9 all-gather.15
  81.4 48.4 all-gather.17
  132.1 40.9 all-gather.19
  175.2 54.8 all-gather.21
  232.1 53.6 all-gather.23
  731.1 69.8 reduce-scatter.9
  814.2 72.1 reduce-scatter.7
  889.8 77.8 reduce-scatter.13
  971.1 77.6 reduce-scatter.11
  1052.1 82.4 reduce-scatter.5
  1137.7 46.6 all-reduce.16
where the time goes:
time: 1210 us; the launch traced here: 1200 us
  waiting for transfers between devices  469 us (39%)
  matrix products  230 us (19%)
  blocking collectives  214 us (18%)
  local copies, waits for them, and re-layouts  101 us (8%)
  other arithmetic  99.3 us (8%)
  starting transfers between devices  61.2 us (5%)
  between operations  23.3 us (2%)
    unnamed x2, blocking collectives  122 us
    reduce_scatter x1, waiting for transfers between devices, on_device(): lax.psum_scatter(grad_sums[0].astype(jnp.bfloat16), 'dp', scatter_dimensi...  85.8 us
    reduce_scatter x1, waiting for transfers between devices, on_device(): lax.psum_scatter(grad_sums[6].astype(jnp.bfloat16), 'dp', scatter_dimensi...  74.3 us
    all_to_all x3, waiting for transfers between devices, layer_forward(): lax.all_to_all(projected, 'seq', split_axis=3, concat_axis=1, tiled=True)  57.6 us
    all_gather x1, waiting for transfers between devices, on_device(): lax.all_gather(contract_weight[0], 'dp', axis=0, tiled=True)  50.2 us
    all_to_all x2, waiting for transfers between devices, layer_backward(): lax.all_to_all(projected_grad, 'seq', split_axis=1, concat_axis=3, tiled=...  39.6 us
    all_gather x1, waiting for transfers between devices, on_device(): lax.all_gather(expand_weight[0], 'dp', axis=0, tiled=True)  36.2 us
    all_gather x1, waiting for transfers between devices, on_device(): lax.all_gather(projection_weight[0], 'dp', axis=0, tiled=True)  34.6 us
  transfers between devices with their start and end apart: 24, of which 19 were waited for; matrix products, arithmetic and copies ran while one was open for 16% of the time, Pallas kernels for 0%

commit v1 on v0

v1 whole, which is shorter than its diff:
```python
import functools

import jax
import jax.numpy as jnp
from jax import lax
from jax.experimental import pallas as pl
from jax.experimental.pallas import tpu as pltpu
from jax.sharding import PartitionSpec as P

HEAD = 64


MESH = pl.DeviceIdType.MESH
ROWS = 608
HALF = ROWS // 2
TOP = 160
LOW = HALF - TOP
WIDE = 768
OFFSETS = (0, 3, 1, 2)


class Place:
    def __init__(self):
        self.s = lax.axis_index("section")
        self.d = lax.axis_index("dp")
        self.q = lax.axis_index("seq")
        y, z = self.d // 4, lax.rem(self.d, 4)
        self.xl, self.c = self.q // 2, lax.rem(self.q, 2)
        self.a = (1 - self.c) * z + self.c * y
        self.b = (1 - self.c) * y + self.c * z

    def dp(self, ka, kb):
        aa = lax.rem(self.a + ka, 4)
        bb = lax.rem(self.b + kb, 4)
        return aa * (1 + 3 * self.c) + bb * (4 - 3 * self.c)

    def ring(self, ka, kb):
        return (self.s, self.dp(ka, kb), self.q)

    def sibling(self):
        return (self.s, self.d, self.xl * 2 + 1 - self.c)

    def across(self):
        return (1 - self.s, self.d, (1 - self.xl) * 2 + self.c)

    def beside(self):
        return (self.s, self.d, (1 - self.xl) * 2 + self.c)

    def askew(self):
        return (self.s, self.d, (1 - self.xl) * 2 + 1 - self.c)

    def flipped(self):
        return (1 - self.s, self.d, self.q)

    def grid_peers(self):
        return [self.ring(k, 0) for k in (1, 3, 2)] + [self.ring(0, k) for k in (1, 3, 2)]


def greet(devices):
    barrier = pltpu.get_barrier_semaphore()
    for device in devices:
        pl.semaphore_signal(barrier, inc=1, device_id=device, device_id_type=MESH)
    pl.semaphore_wait(barrier, len(devices))


def half_rows(core, offset, count):
    return pl.ds(pl.multiple_of(core * HALF + offset, 16), count)


class Wires:
    def __init__(self, send, recv):
        self.send, self.recv, self.started = send, recv, []

    def push(self, index, source, target, device, landing=None):
        item = pltpu.make_async_remote_copy(
            src_ref=source,
            dst_ref=target,
            send_sem=self.send.at[index],
            recv_sem=self.recv.at[index if landing is None else landing],
            device_id=device,
            device_id_type=MESH,
        )
        item.start()
        self.started.append(item)

    def got(self, index, target, device):
        pltpu.make_async_remote_copy(
            src_ref=target,
            dst_ref=target,
            send_sem=self.send.at[0],
            recv_sem=self.recv.at[index],
            device_id=device,
            device_id_type=MESH,
        ).wait_recv()

    def finish(self):
        for item in self.started:
            item.wait_send()


TOKENS = 256
PAIR = 128
EXPAND_ROWS = (192, 240, 304, 352)
CONTRACT_ROW = 400
BIAS_ROW = 288
ROOT = (2.0 / 3.141592653589793) ** 0.5


def norm_rows(values):
    row_mean = jnp.mean(values, axis=-1, keepdims=True)
    centered = values - row_mean
    variance = jnp.mean(centered * centered, axis=-1, keepdims=True)
    inv_std = lax.rsqrt(variance + 1e-06)
    return (centered * inv_std, inv_std)


def norm_back(gradient, normed, inv_std):
    row_mean = jnp.mean(gradient, axis=-1, keepdims=True)
    along = jnp.mean(gradient * normed, axis=-1, keepdims=True)
    return inv_std * (gradient - row_mean - normed * along)


def dot(left, right, left_dim=1, right_dim=0):
    return lax.dot_general(
        left, right, (((left_dim,), (right_dim,)), ((), ())), preferred_element_type=jnp.float32
    )


def column_sum(values):
    return jnp.sum(values.astype(jnp.float32), axis=0, keepdims=True)


def square(w, row):
    return w[:, row : row + 48, :].reshape(WIDE, WIDE)


def contract_square(w, part):
    return w[4 * part : 4 * part + 4, CONTRACT_ROW : CONTRACT_ROW + 192, :].reshape(WIDE, WIDE)


def side_by_side(ref, lead=()):
    return jnp.concatenate([ref[(*lead, pair)] for pair in range(6)], axis=1)


def head_lanes(head):
    lane = lax.broadcasted_iota(jnp.int32, (1, PAIR), 1)
    return (lane // HEAD) == head


def only_head(values, head):
    return jnp.where(head_lanes(head), values, jnp.zeros_like(values))


def gather_steps(me, wires, base, source, w_ref, local):
    right_a, left_a = me.ring(1, 0), me.ring(3, 0)
    right_b, left_b = me.ring(0, 1), me.ring(0, 3)
    sibling = me.sibling()

    def slot(ka, kb, offset=0, count=HALF):
        return w_ref.at[me.dp(ka, kb), half_rows(me.c, offset, count), :]

    def got(index, target):
        wires.got(base + index, target, sibling)

    def push(index, origin, target, device):
        wires.push(base + index, origin, target, device)

    def to_side(ka, kb, origin=None):
        block = slot(ka, kb)
        push(20 + 4 * ka + kb, block if origin is None else origin, block, sibling)

    def spread_b(ka, origin=None):
        block = slot(ka, 0)
        origin = block if origin is None else origin
        push(4 + 4 * ka, origin, block, right_b)
        push(5 + 4 * ka, origin, block, left_b)

    own = pltpu.make_async_copy(source, slot(0, 0), local)

    def start():
        own.start()
        push(0, source, slot(0, 0), right_a)
        push(1, source, slot(0, 0), left_a)
        spread_b(0, source)
        to_side(0, 0, source)

    def forward_a():
        got(0, slot(3, 0))
        push(2, slot(3, 0, 0, TOP), slot(3, 0, 0, TOP), right_a)
        spread_b(3)
        to_side(3, 0)
        got(1, slot(1, 0))
        push(3, slot(1, 0, TOP, LOW), slot(1, 0, TOP, LOW), left_a)
        spread_b(1)
        to_side(1, 0)

    def end_a():
        got(2, slot(2, 0, 0, TOP))
        got(3, slot(2, 0, TOP, LOW))
        spread_b(2)
        to_side(2, 0)

    def forward_b(ka):
        at = 4 + 4 * ka
        got(at, slot(ka, 3))
        push(at + 2, slot(ka, 3, 0, TOP), slot(ka, 3, 0, TOP), right_b)
        to_side(ka, 3)
        got(at + 1, slot(ka, 1))
        push(at + 3, slot(ka, 1, TOP, LOW), slot(ka, 1, TOP, LOW), left_b)
        to_side(ka, 1)

    def end_b(ka):
        at = 4 + 4 * ka
        got(at + 2, slot(ka, 2, 0, TOP))
        got(at + 3, slot(ka, 2, TOP, LOW))
        to_side(ka, 2)

    def finish():
        own.wait()
        for ka in range(4):
            for kb in range(4):
                got(20 + 4 * ka + kb, w_ref.at[me.dp(kb, ka), half_rows(1 - me.c, 0, HALF), :])

    steps = [start, forward_a, end_a]
    steps += [functools.partial(forward_b, ka) for ka in OFFSETS]
    steps += [functools.partial(end_b, ka) for ka in OFFSETS]
    return steps + [finish]


def swap_steps(me, wires, base, pieces, first, second, result):
    def start():
        for ka in range(4):
            for kb in range(4):
                first[0, ka, kb] = pieces[me.dp(ka, kb)]
        for k in (1, 2, 3):
            wires.push(base + k - 1, first.at[0, k], first.at[1, k], me.ring(k, 0))

    def middle():
        for kb in range(4):
            second[0, kb, 0] = first[0, 0, kb]
        for k in (1, 2, 3):
            wires.got(base + k - 1, first.at[1, k], me.sibling())
            for kb in range(4):
                second[0, kb, k] = first[1, k, kb]
        for k in (1, 2, 3):
            wires.push(base + 2 + k, second.at[0, k], second.at[1, k], me.ring(0, k))

    def end():
        for ka in range(4):
            result[me.dp((4 - ka) % 4, 0)] = second[0, 0, ka]
        for k in (1, 2, 3):
            wires.got(base + 2 + k, second.at[1, k], me.sibling())
            for ka in range(4):
                result[me.dp((4 - ka) % 4, 4 - k)] = second[1, k, ka]

    return [start, middle, end]


def modulation_steps(me, wires, base, conds_ref, weight_ref, columns_ref, mod_ref, first, second, partial, b_sums, a_sums, across_sums):
    swap = swap_steps(me, wires, base, conds_ref, first, second, columns_ref)

    def multiply():
        swap[2]()
        rows = lax.broadcasted_iota(jnp.int32, (8, 32), 0)
        taken = lax.broadcasted_iota(jnp.int32, (8, 32), 1)
        pick = jnp.where(taken == (rows // 2) * 8 + lax.rem(rows, 2), 1.0, 0.0).astype(jnp.bfloat16)
        for kb in range(4):
            found = jnp.concatenate([columns_ref[me.dp((4 - ka) % 4, (4 - kb) % 4)] for ka in range(4)], axis=0)
            silu = (found / (1.0 + jnp.exp(-found))).astype(jnp.bfloat16)
            silu = dot(pick, silu).astype(jnp.bfloat16)
            partial[kb] = dot(silu, weight_ref[...])
        for k in (1, 2, 3):
            wires.push(base + 5 + k, partial.at[k], b_sums.at[k - 1], me.ring(0, 4 - k))

    def add_b():
        for k in (1, 2, 3):
            wires.got(base + 5 + k, b_sums.at[k - 1], me.sibling())
        a_sums[0] = partial[0] + b_sums[0] + b_sums[1] + b_sums[2]
        for k in (1, 2, 3):
            wires.push(base + 8 + k, a_sums.at[0], a_sums.at[k], me.ring(4 - k, 0))

    def add_a():
        for k in (1, 2, 3):
            wires.got(base + 8 + k, a_sums.at[k], me.sibling())
        total = a_sums[0, 0:2]
        for k in (1, 2, 3):
            total = total + a_sums[k, 2 * k : 2 * k + 2]
        across_sums[0] = jnp.concatenate([total, jnp.zeros((6, total.shape[1]), jnp.float32)], axis=0)
        wires.push(base + 12, across_sums.at[0], across_sums.at[1], me.flipped())

    def end():
        wires.got(base + 12, across_sums.at[1], me.sibling())
        lead = me.s == 0
        kept = jnp.where(lead, across_sums[0, 0:1], across_sums[0, 1:2])
        came = jnp.where(lead, across_sums[1, 0:1], across_sums[1, 1:2])
        zeros = jnp.zeros((2, WIDE), jnp.float32)
        for block, row in ((0, jnp.where(lead, kept, came)), (1, jnp.where(lead, came, kept))):
            mod_ref[block] = jnp.concatenate([row[:, r * WIDE : (r + 1) * WIDE] for r in range(6)] + [zeros], axis=0)

    return [swap[0], swap[1], multiply, add_b, add_a, end]


def gather_kernel(p_ref, conds_ref, weight_ref, first_ref, second_ref, columns_ref, mod_ref, shard, c_first, c_second, partial, b_sums, a_sums, across_sums, local, send, recv):
    me = Place()
    mine = p_ref.at[half_rows(me.c, 0, HALF), :]
    own = pltpu.make_async_copy(mine, shard.at[me.s], local.at[2])
    own.start()
    greet(me.grid_peers() + [me.across(), me.flipped(), me.sibling()])
    wires = Wires(send, recv)
    wires.push(0, mine, shard.at[me.s], me.across())
    small = modulation_steps(me, wires, 73, conds_ref, weight_ref, columns_ref, mod_ref, c_first, c_second, partial, b_sums, a_sums, across_sums)
    small[0]()
    small[1]()
    own.wait()
    wires.got(0, shard.at[1 - me.s], me.across())
    one = gather_steps(me, wires, 1, shard.at[0], first_ref, local.at[0])
    two = gather_steps(me, wires, 37, shard.at[1], second_ref, local.at[1])
    one[0]()
    two[0]()
    small[2]()
    one[1]()
    small[3]()
    one[2]()
    two[1]()
    small[4]()
    two[2]()
    small[5]()
    for step in one[3:7] + two[3:7] + one[7:11] + two[7:11] + [one[11], two[11]]:
        step()
    wires.finish()


def gather_weights(packed, conds, weight):
    bf, f32 = jnp.bfloat16, jnp.float32
    wide = weight.shape[1]
    whole = pl.BlockSpec(memory_space=pltpu.VMEM)
    away = pl.BlockSpec(memory_space=pl.ANY)
    return pl.pallas_call(
        gather_kernel,
        out_shape=[
            jax.ShapeDtypeStruct((16, ROWS, WIDE), bf),
            jax.ShapeDtypeStruct((16, ROWS, WIDE), bf),
            jax.ShapeDtypeStruct((16, 8, PAIR), f32),
            jax.ShapeDtypeStruct((2, 8, WIDE), f32),
        ],
        in_specs=[away, whole, whole],
        out_specs=[away, away, whole, whole],
        scratch_shapes=[
            pltpu.VMEM((2, HALF, WIDE), bf),
            pltpu.VMEM((2, 4, 4, 8, PAIR), f32),
            pltpu.VMEM((2, 4, 4, 8, PAIR), f32),
            pltpu.VMEM((4, 8, wide), f32),
            pltpu.VMEM((3, 8, wide), f32),
            pltpu.VMEM((4, 8, wide), f32),
            pltpu.VMEM((2, 8, wide), f32),
            pltpu.SemaphoreType.DMA((3,)),
            pltpu.SemaphoreType.DMA((86,)),
            pltpu.SemaphoreType.DMA((86,)),
        ],
        compiler_params=pltpu.CompilerParams(
            collective_id=0, has_side_effects=True, vmem_limit_bytes=24 * 1024 * 1024
        ),
        cost_estimate=pl.CostEstimate(flops=0, bytes_accessed=60000000, transcendentals=0),
        name="gather_weights",
    )(packed, conds, weight)


def reduce_steps(me, wires, base, source, load, buffers):
    mine, sib, r_top, r_low, r_left, r_right, a_top, a_low, a_left, a_right = buffers
    right_a, left_a = me.ring(1, 0), me.ring(3, 0)
    right_b, left_b = me.ring(0, 1), me.ring(0, 3)
    sibling = me.sibling()

    def push(index, origin, target, device):
        wires.push(base + index, origin, target, device)

    def got(index, target):
        wires.got(base + index, target, sibling)

    def block(ka, kb):
        return mine.at[me.dp(ka, kb)]

    def from_side(ka, kb):
        return sib.at[me.dp(ka, kb)]

    def fetch(ka, kb):
        dp = me.dp(ka, kb)
        return pltpu.make_async_copy(source.at[dp, half_rows(me.c, 0, HALF), :], mine.at[dp], load.at[4 * ka + kb])

    def start():
        for kb in (2, 1, 3, 0):
            for ka in (2, 1, 3, 0):
                fetch(ka, kb).start()
                dp = me.dp(kb, ka)
                push(4 * ka + kb, source.at[dp, half_rows(1 - me.c, 0, HALF), :], sib.at[dp], sibling)

    def total(target, parts, offset=0, count=HALF):
        add_rows(target, parts, offset, count)

    def ready(ka, kb):
        fetch(ka, kb).wait()
        got(4 * ka + kb, from_side(ka, kb))

    def far_b(ka):
        ready(ka, 2)
        far = block(ka, 2)
        total(far, [(from_side(ka, 2), 0)])
        push(16 + 4 * ka, far.at[pl.ds(0, TOP), :], r_top.at[ka], right_b)
        push(17 + 4 * ka, far.at[pl.ds(TOP, LOW), :], r_low.at[ka], left_b)

    def near_b(ka):
        at = 16 + 4 * ka
        ready(ka, 1)
        got(at, r_top.at[ka])
        near, side = block(ka, 1), from_side(ka, 1)
        total(near, [(side, 0), (r_top.at[ka], 0)], 0, TOP)
        total(near, [(side, 0)], TOP, LOW)
        push(at + 2, near, r_left.at[ka], right_b)
        ready(ka, 3)
        got(at + 1, r_low.at[ka])
        near, side = block(ka, 3), from_side(ka, 3)
        total(near, [(side, 0)], 0, TOP)
        total(near, [(side, 0), (r_low.at[ka], TOP)], TOP, LOW)
        push(at + 3, near, r_right.at[ka], left_b)

    def own_b(ka):
        at = 16 + 4 * ka
        ready(ka, 0)
        got(at + 2, r_left.at[ka])
        got(at + 3, r_right.at[ka])
        total(block(ka, 0), [(from_side(ka, 0), 0), (r_left.at[ka], 0), (r_right.at[ka], 0)])
        if ka == 2:
            far = block(2, 0)
            push(32, far.at[pl.ds(0, TOP), :], a_top, right_a)
            push(33, far.at[pl.ds(TOP, LOW), :], a_low, left_a)

    def near_a():
        got(32, a_top)
        total(block(1, 0), [(a_top, 0)], 0, TOP)
        push(34, block(1, 0), a_left, right_a)
        got(33, a_low)
        total(block(3, 0), [(a_low, TOP)], TOP, LOW)
        push(35, block(3, 0), a_right, left_a)

    def own_a():
        got(34, a_left)
        got(35, a_right)
        total(block(0, 0), [(a_left, 0), (a_right, 0)])

    order = (2, 1, 3, 0)
    steps = [start]
    for made in (far_b, near_b, own_b):
        steps += [functools.partial(made, ka) for ka in order]
    return steps + [near_a, own_a]


def add_rows(target, parts, offset=0, count=HALF):
    def step(i, carry):
        rows = pl.ds(pl.multiple_of(offset + 16 * i, 16), 16)
        value = target[rows, :].astype(jnp.float32)
        for part, start in parts:
            value = value + part[pl.ds(pl.multiple_of(offset - start + 16 * i, 16), 16), :].astype(jnp.float32)
        target[rows, :] = value.astype(jnp.bfloat16)
        return carry

    lax.fori_loop(0, count // 16, step, 0)


def terms_steps(me, wires, base, first_ref, second_ref, weight_ref, all_ref, conds_ref, sums, rounded, tiles, c_first, c_second):
    peers = [me.sibling(), me.beside(), me.askew()]

    def start():
        sums[me.q, 0] = first_ref[...]
        sums[me.q, 1] = second_ref[...]
        for k in range(3):
            wires.push(base + k, sums.at[me.q], sums.at[me.q], peers[k], base + k)

    def add():
        for k in range(3):
            wires.got(base + k, sums.at[peers[k][2]], peers[k])
        total = sums[0] + sums[1] + sums[2] + sums[3]
        rounded[...] = total.astype(jnp.bfloat16).astype(jnp.float32)
        all_ref[me.d, me.s] = rounded[me.s]
        wires.push(base + 3, rounded.at[1 - me.s], all_ref.at[me.d, me.s], me.flipped())

    def spread_a():
        wires.got(base + 3, all_ref.at[me.d, 1 - me.s], me.sibling())
        for k in (1, 2, 3):
            wires.push(base + 3 + k, all_ref.at[me.d], all_ref.at[me.d], me.ring(k, 0))

    def spread_b():
        for k in (1, 2, 3):
            wires.got(base + 3 + k, all_ref.at[me.dp(4 - k, 0)], me.sibling())
        for ka in range(4):
            block = all_ref.at[me.dp((4 - ka) % 4, 0)]
            for k in (1, 2, 3):
                wires.push(base + 4 + 3 * ka + 2 + k, block, block, me.ring(0, k))

    def multiply():
        for ka in range(4):
            for k in (1, 2, 3):
                wires.got(base + 4 + 3 * ka + 2 + k, all_ref.at[me.dp((4 - ka) % 4, 4 - k)], me.sibling())
        grads = all_ref[...].reshape(256, WIDE).astype(jnp.bfloat16)
        row = lax.rem(lax.broadcasted_iota(jnp.int32, (256, PAIR), 0), 8)
        total = jnp.zeros((256, PAIR), jnp.float32)
        for r in range(6):
            made = dot(grads, weight_ref[:, r * WIDE : (r + 1) * WIDE], 1, 1)
            total = total + jnp.where(row == r, made, 0.0)
        total = jnp.sum(total.reshape(16, 2, 8, PAIR), axis=2, keepdims=True)
        level = lax.broadcasted_iota(jnp.int32, (16, 8, PAIR), 1)
        tiles[0] = jnp.where(level == 0, total[:, 0], jnp.where(level == 1, total[:, 1], 0.0))
        wires.push(base + 19, tiles.at[0], tiles.at[1], me.flipped())

    def join():
        wires.got(base + 19, tiles.at[1], me.sibling())
        tiles[2] = tiles[0] + tiles[1]
        swap_two[0]()

    swap_two = swap_steps(me, wires, base + 20, tiles.at[2], c_first, c_second, conds_ref)
    return [start, add, spread_a, spread_b, multiply, join, swap_two[1], swap_two[2]]


def reduce_kernel(
    first_ref, second_ref, first_terms, second_terms, weight_ref, kept_out, sent_out, kept_grad, sent_grad,
    o_ref, all_ref, conds_ref, outs_ref, grads_ref,
    mine, sib, r_top, r_low, r_left, r_right, a_top, a_low, a_left, a_right, r_across, r_beside,
    sums, rounded, tiles, c_first, c_second, load, local, send, recv,
):
    me = Place()
    greet(me.grid_peers() + [me.across(), me.flipped(), me.beside(), me.askew(), me.sibling()])
    wires = Wires(send, recv)
    buffers = (mine, sib, r_top, r_low, r_left, r_right, a_top, a_low, a_left, a_right)
    one = reduce_steps(me, wires, 0, second_ref, load.at[1], [ref.at[1] for ref in buffers])
    two = reduce_steps(me, wires, 36, first_ref, load.at[0], [ref.at[0] for ref in buffers])
    small = terms_steps(me, wires, 77, first_terms, second_terms, weight_ref, all_ref, conds_ref, sums, rounded, tiles, c_first, c_second)
    one[0]()
    two[0]()
    small[0]()
    keeps = [
        pltpu.make_async_copy(kept_out, outs_ref.at[me.s], local.at[0]),
        pltpu.make_async_copy(kept_grad, grads_ref.at[me.s], local.at[1]),
    ]
    for item in keeps:
        item.start()
    wires.push(72, sent_out, outs_ref.at[me.s], me.flipped())
    wires.push(73, sent_grad, grads_ref.at[me.s], me.flipped())
    big = one[1:5] + two[1:5] + one[5:9] + two[5:9] + one[9:13] + two[9:13] + [one[13], two[13], one[14], two[14]]
    small = small[1:]
    for index, step in enumerate(big):
        step()
        if index % 3 == 2 and small:
            small.pop(0)()
    while small:
        small.pop(0)()
    held = mine.at[me.s, me.d]
    wires.push(74, mine.at[1 - me.s, me.d], r_across, me.across())
    wires.got(74, r_across, me.across())
    add_rows(held, [(r_across, 0)])
    beside = pltpu.make_async_remote_copy(
        src_ref=held, dst_ref=r_beside, send_sem=send.at[75], recv_sem=recv.at[75], device_id=me.beside(), device_id_type=MESH
    )
    beside.start()
    wires.got(75, r_beside, me.beside())
    beside.wait_send()
    add_rows(held, [(r_beside, 0)])
    out_rows = o_ref.at[half_rows(me.c, 0, HALF), :]
    wires.push(76, held, out_rows, me.sibling())
    own = pltpu.make_async_copy(held, out_rows, local.at[2])
    own.start()
    own.wait()
    for item in keeps:
        item.wait()
    wires.got(72, outs_ref.at[1 - me.s], me.flipped())
    wires.got(73, grads_ref.at[1 - me.s], me.flipped())
    wires.got(76, o_ref.at[half_rows(1 - me.c, 0, HALF), :], me.sibling())
    wires.finish()


def reduce_grads(*operands):
    count = 77 + 26
    bf, f32 = jnp.bfloat16, jnp.float32
    blocks = lambda *lead: pltpu.VMEM(lead + (WIDE,), bf)
    whole = pl.BlockSpec(memory_space=pltpu.VMEM)
    away = pl.BlockSpec(memory_space=pl.ANY)
    return pl.pallas_call(
        reduce_kernel,
        out_shape=[
            jax.ShapeDtypeStruct((ROWS, WIDE), bf),
            jax.ShapeDtypeStruct((16, 2, 8, WIDE), f32),
            jax.ShapeDtypeStruct((16, 8, PAIR), f32),
            jax.ShapeDtypeStruct((2, TOKENS, WIDE), bf),
            jax.ShapeDtypeStruct((2, TOKENS, WIDE), f32),
        ],
        in_specs=[away, away, whole, whole, whole, away, away, away, away],
        out_specs=[away, whole, whole, away, away],
        scratch_shapes=[
            blocks(2, 16, HALF),
            blocks(2, 16, HALF),
            blocks(2, 4, TOP),
            blocks(2, 4, LOW),
            blocks(2, 4, HALF),
            blocks(2, 4, HALF),
            blocks(2, TOP),
            blocks(2, LOW),
            blocks(2, HALF),
            blocks(2, HALF),
            blocks(HALF),
            blocks(HALF),
            pltpu.VMEM((4, 2, 8, WIDE), f32),
            pltpu.VMEM((2, 8, WIDE), f32),
            pltpu.VMEM((3, 16, 8, PAIR), f32),
            pltpu.VMEM((2, 4, 4, 8, PAIR), f32),
            pltpu.VMEM((2, 4, 4, 8, PAIR), f32),
            pltpu.SemaphoreType.DMA((2, 16)),
            pltpu.SemaphoreType.DMA((3,)),
            pltpu.SemaphoreType.DMA((count,)),
            pltpu.SemaphoreType.DMA((count,)),
        ],
        compiler_params=pltpu.CompilerParams(
            collective_id=1, has_side_effects=True, vmem_limit_bytes=57 * 1024 * 1024
        ),
        cost_estimate=pl.CostEstimate(flops=0, bytes_accessed=60000000, transcendentals=0),
        name="reduce_grads",
    )(*operands)


def seq_peers(me):
    far = [(me.s, me.d, (1 - me.xl) * 2 + core) for core in range(2)]
    return me.sibling(), far


def forward_kernel(
    part, x_ref, mod_ref, bias_ref, w_hbm,
    out_ref, mixed_one_ref, qkv_out, lse_ref, att_out, branch_one_ref, middle_ref, mixed_two_ref, expanded_out, branch_two_ref,
    w, stage, qkv, heads, att, expanded, load, save, send, recv,
):
    me = Place()
    sibling, far = seq_peers(me)
    first_load = pltpu.make_async_copy(w_hbm.at[:, pl.ds(0, 144), :], w.at[:, pl.ds(0, 144), :], load.at[0])
    rest_load = pltpu.make_async_copy(w_hbm.at[:, pl.ds(144, 464), :], w.at[:, pl.ds(144, 464), :], load.at[1])
    first_load.start()
    rest_load.start()
    greet([sibling, *far])
    wires = Wires(send, recv)

    row = lambda index: mod_ref[index : index + 1, :]
    bias = lambda index: bias_ref[index : index + 1, :]
    tokens = x_ref[...].astype(jnp.float32)
    normed_one, _ = norm_rows(tokens)
    mixed_one = (normed_one * (1.0 + row(1)) + row(0)).astype(jnp.bfloat16)
    mixed_one_ref[...] = mixed_one
    first_load.wait()

    def project(kind, weight_row, added):
        made = dot(mixed_one, square(w, weight_row))
        if added is not None:
            made = made + added
        made = made.astype(jnp.bfloat16)
        for pair in range(6):
            stage[pair, kind] = made[:, pair * PAIR : (pair + 1) * PAIR]

    project(0, 48, None)
    project(1, 96, bias(1))
    for j in range(3):
        for g in range(2):
            wires.push(2 * j + g, stage.at[3 * g + j, pl.ds(0, 2)], qkv.at[2 + me.c, j, pl.ds(0, 2)], far[g], 2 * j + me.c)
    project(2, 0, bias(0))
    for j in range(3):
        wires.push(6 + j, stage.at[3 * (1 - me.c) + j], qkv.at[me.c, j], sibling)
    for j in range(3):
        qkv[me.c, j] = stage[3 * me.c + j]

    for j in range(3):
        wires.got(6 + j, qkv.at[1 - me.c, j], sibling)
        for g in range(2):
            wires.got(2 * j + g, qkv.at[2 + g, j, pl.ds(0, 2)], far[g])

        def queries_step(g, carry):
            keys = qkv[:, j, 0].reshape(4 * TOKENS, PAIR)
            values = qkv[:, j, 1].reshape(4 * TOKENS, PAIR)
            queries = qkv[g, j, 2] * jnp.bfloat16(0.125)
            made = []
            for head in range(2):
                scores = dot(keys, only_head(queries, head), 1, 1)
                top = jnp.max(scores, axis=0, keepdims=True)
                powers = jnp.exp(scores - top)
                sums = jnp.sum(powers, axis=0, keepdims=True)
                lse_ref[(2 * j + head) * 2 + g] = top + jnp.log(sums)
                weights = (powers * (1.0 / sums)).astype(jnp.bfloat16)
                made.append(dot(values, weights, 0, 0)[head * HEAD : (head + 1) * HEAD])
            heads[g, j] = jnp.concatenate(made, axis=0).T.astype(jnp.bfloat16)
            return carry

        lax.fori_loop(0, 2, queries_step, 0)
        wires.push(9 + j, heads.at[1 - me.c, j], att.at[3 * me.c + j], sibling)
        att[3 * me.c + j] = heads[me.c, j]
    qkv_save = pltpu.make_async_copy(qkv, qkv_out, save.at[0])
    qkv_save.start()
    rest_load.wait()
    for j in range(3):
        wires.got(9 + j, att.at[3 * (1 - me.c) + j], sibling)
    att_save = pltpu.make_async_copy(att, att_out, save.at[1])
    att_save.start()
    attended = side_by_side(att)
    branch_one = dot(attended, square(w, 144)) + bias(2)
    branch_one_ref[...] = branch_one
    middle = tokens + row(2) * branch_one
    middle_ref[...] = middle
    normed_two, _ = norm_rows(middle)
    mixed_two = (normed_two * (1.0 + row(4)) + row(3)).astype(jnp.bfloat16)
    mixed_two_ref[...] = mixed_two
    total = bias(7)
    saves = []
    for k in range(4):
        u = dot(mixed_two, square(w, EXPAND_ROWS[k])) + bias(3 + k)
        expanded[k] = u
        item = pltpu.make_async_copy(expanded.at[k], expanded_out.at[k], save.at[2 + k])
        item.start()
        saves.append(item)
        activated = (0.5 * u * (1.0 + jnp.tanh(ROOT * (u + 0.044715 * (u * u * u))))).astype(jnp.bfloat16)
        total = total + dot(activated, contract_square(w, k))
    branch_two_ref[...] = total
    out_ref[...] = (middle + row(5) * total).astype(jnp.bfloat16)
    qkv_save.wait()
    att_save.wait()
    for item in saves:
        item.wait()
    wires.finish()


def block_forward(part, tokens, modulation, bias, blocks):
    shape = lambda dims, dtype: jax.ShapeDtypeStruct(dims, dtype)
    bf, f32 = jnp.bfloat16, jnp.float32
    whole = pl.BlockSpec(memory_space=pltpu.VMEM)
    away = pl.BlockSpec(memory_space=pl.ANY)
    return pl.pallas_call(
        functools.partial(forward_kernel, part),
        out_shape=[
            shape((TOKENS, WIDE), bf),
            shape((TOKENS, WIDE), bf),
            shape((4, 3, 3, TOKENS, PAIR), bf),
            shape((12, 1, TOKENS), f32),
            shape((6, TOKENS, PAIR), bf),
            shape((TOKENS, WIDE), f32),
            shape((TOKENS, WIDE), f32),
            shape((TOKENS, WIDE), bf),
            shape((4, TOKENS, WIDE), f32),
            shape((TOKENS, WIDE), f32),
        ],
        in_specs=[whole, whole, whole, away],
        out_specs=[whole, whole, away, whole, away, whole, whole, whole, away, whole],
        scratch_shapes=[
            pltpu.VMEM((16, ROWS, WIDE), bf),
            pltpu.VMEM((6, 3, TOKENS, PAIR), bf),
            pltpu.VMEM((4, 3, 3, TOKENS, PAIR), bf),
            pltpu.VMEM((2, 3, TOKENS, PAIR), bf),
            pltpu.VMEM((6, TOKENS, PAIR), bf),
            pltpu.VMEM((4, TOKENS, WIDE), f32),
            pltpu.SemaphoreType.DMA((2,)),
            pltpu.SemaphoreType.DMA((6,)),
            pltpu.SemaphoreType.DMA((12,)),
            pltpu.SemaphoreType.DMA((12,)),
        ],
        compiler_params=pltpu.CompilerParams(
            collective_id=2 + part, has_side_effects=True, vmem_limit_bytes=56 * 1024 * 1024
        ),
        cost_estimate=pl.CostEstimate(flops=5 * 10**9, bytes_accessed=25 * 10**6, transcendentals=4 * 10**6),
        name=("forward_first", "forward_second")[part],
    )(tokens, modulation, bias, blocks)


def backward_kernel(
    part, grad_ref, x_ref, mod_ref, w_hbm, mixed_one_ref, qkv_in, lse_ref, att_ref, branch_one_ref, middle_ref, mixed_two_ref, expanded_in, branch_two_ref,
    input_grad_ref, terms_ref, grads_out,
    w, made, expanded, qkv, stage, given, dkv, dq, own, far_out, far_in, side_out, side_in, joined, load, save, send, recv,
):
    me = Place()
    sibling, far = seq_peers(me)
    c, other = me.c, 1 - me.c
    back_load = pltpu.make_async_copy(w_hbm.at[:, pl.ds(192, 416), :], w.at[:, pl.ds(192, 416), :], load.at[0])
    expanded_load = pltpu.make_async_copy(expanded_in, expanded, load.at[1])
    front_load = pltpu.make_async_copy(w_hbm.at[:, pl.ds(0, 192), :], w.at[:, pl.ds(0, 192), :], load.at[2])
    qkv_load = pltpu.make_async_copy(qkv_in, qkv, load.at[3])
    back_load.start()
    expanded_load.start()
    front_load.start()
    qkv_load.start()
    greet([sibling, *far])
    wires = Wires(send, recv)
    saves = []

    def keep(index, start, count):
        rows = pl.ds(start, count)
        item = pltpu.make_async_copy(made.at[:, rows, :], grads_out.at[:, rows, :], save.at[index])
        item.start()
        saves.append(item)

    row = lambda index: mod_ref[index : index + 1, :]
    gradient = grad_ref[...].astype(jnp.float32)
    branch_two_grad = (row(5) * gradient).astype(jnp.bfloat16)
    gate_two_grad = column_sum(gradient * branch_two_ref[...])
    contract_bias_grad = column_sum(branch_two_grad)
    mixed_two = mixed_two_ref[...]
    mixed_two_grad = None
    expand_bias_grads = []
    back_load.wait()
    expanded_load.wait()
    for k in range(4):
        u = expanded[k]
        squared = u * u
        tanh = jnp.tanh(ROOT * (u + 0.044715 * (squared * u)))
        half = 0.5 * (1.0 + tanh)
        activated = (u * half).astype(jnp.bfloat16)
        slope = half + 0.5 * u * (1.0 - tanh * tanh) * (ROOT * (1.0 + (3.0 * 0.044715) * squared))
        made[4 * k : 4 * k + 4, CONTRACT_ROW : CONTRACT_ROW + 192, :] = (
            dot(activated, branch_two_grad, 0, 0).astype(jnp.bfloat16).reshape(4, 192, WIDE)
        )
        expanded_grad = (dot(branch_two_grad, contract_square(w, k), 1, 1) * slope).astype(jnp.bfloat16)
        start = EXPAND_ROWS[k]
        made[:, start : start + 48, :] = dot(mixed_two, expanded_grad, 0, 0).astype(jnp.bfloat16).reshape(16, 48, WIDE)
        expand_bias_grads.append(column_sum(expanded_grad))
        term = dot(expanded_grad, square(w, start), 1, 1)
        mixed_two_grad = term if mixed_two_grad is None else mixed_two_grad + term
    keep(0, 304, 288)
    keep(1, 192, 96)
    normed_two, inv_two = norm_rows(middle_ref[...])
    scale_two_grad = column_sum(mixed_two_grad * normed_two)
    shift_two_grad = column_sum(mixed_two_grad)
    middle_grad = gradient + norm_back(mixed_two_grad * (1.0 + row(4)), normed_two, inv_two)
    gate_one_grad = column_sum(middle_grad * branch_one_ref[...])
    branch_one_grad = (row(2) * middle_grad).astype(jnp.bfloat16)
    front_load.wait()
    attended_grad = dot(branch_one_grad, square(w, 144), 1, 1).astype(jnp.bfloat16)
    for pair in range(6):
        stage[pair] = attended_grad[:, pair * PAIR : (pair + 1) * PAIR]
    wires.push(0, stage.at[pl.ds(3 * other, 3)], given.at[c], sibling)
    given[c] = stage[pl.ds(3 * c, 3)]
    input_grad_ref[...] = middle_grad
    made[:, 144:192, :] = dot(side_by_side(att_ref), branch_one_grad, 0, 0).astype(jnp.bfloat16).reshape(16, 48, WIDE)
    keep(2, 144, 48)
    attention_bias_grad = column_sum(branch_one_grad)
    qkv_load.wait()
    wires.got(0, given.at[other], sibling)

    for j in range(3):
        dkv[...] = jnp.zeros_like(dkv)

        def queries_step(g, carry):
            keys = qkv[:, j, 0].reshape(4 * TOKENS, PAIR)
            values = qkv[:, j, 1].reshape(4 * TOKENS, PAIR)
            queries = qkv[g, j, 2] * jnp.bfloat16(0.125)
            output_grads = given[g, j]
            key_sums, value_sums, query_parts = 0.0, 0.0, []
            for head in range(2):
                head_queries = only_head(queries, head)
                head_grads = only_head(output_grads, head)
                scores = dot(keys, head_queries, 1, 1)
                probs = jnp.exp(scores - lse_ref[(2 * j + head) * 2 + g])
                weight_grads = dot(values, head_grads, 1, 1)
                centre = jnp.sum(probs * weight_grads, axis=0, keepdims=True)
                score_grads = (probs * (weight_grads - centre)).astype(jnp.bfloat16)
                key_sums = key_sums + dot(score_grads, head_queries)
                value_sums = value_sums + dot(probs.astype(jnp.bfloat16), head_grads)
                query_parts.append(dot(keys, score_grads, 0, 0)[head * HEAD : (head + 1) * HEAD])
            dq[g] = jnp.concatenate(query_parts, axis=0).T * 0.125
            dkv[0] += key_sums.reshape(4, TOKENS, PAIR)
            dkv[1] += value_sums.reshape(4, TOKENS, PAIR)
            return carry

        lax.fori_loop(0, 2, queries_step, 0)
        for g in range(2):
            far_out[j, g] = dkv[:, 2 + g].astype(jnp.bfloat16)
            wires.push(1 + 2 * j + g, far_out.at[j, g], far_in.at[j, c], far[g], 1 + 2 * j + c)
        side_out[j, 0:2] = dkv[:, other].astype(jnp.bfloat16)
        side_out[j, 2] = dq[other].astype(jnp.bfloat16)
        wires.push(7 + j, side_out.at[j], side_in.at[j], sibling)
        own[j, 0:2] = dkv[:, c]
        own[j, 2] = dq[c]

    for j in range(3):
        wires.got(7 + j, side_in.at[j], sibling)
        for g in range(2):
            wires.got(1 + 2 * j + g, far_in.at[j, g], far[g])
        for kind in range(2):
            joined[kind, 3 * c + j] = (own[j, kind] + far_in[j, c, kind].astype(jnp.float32)).astype(jnp.bfloat16)
            joined[kind, 3 * other + j] = (
                side_in[j, kind].astype(jnp.float32) + far_in[j, other, kind].astype(jnp.float32)
            ).astype(jnp.bfloat16)
        joined[2, 3 * c + j] = own[j, 2].astype(jnp.bfloat16)
        joined[2, 3 * other + j] = side_in[j, 2]
    mixed_one = mixed_one_ref[...]
    mixed_one_grad, bias_grads = None, []
    for kind, start in ((0, 48), (1, 96), (2, 0)):
        piece = side_by_side(joined, (kind,))
        bias_grads.append(column_sum(piece))
        made[:, start : start + 48, :] = dot(mixed_one, piece, 0, 0).astype(jnp.bfloat16).reshape(16, 48, WIDE)
        term = dot(piece, square(w, start), 1, 1)
        mixed_one_grad = term if mixed_one_grad is None else mixed_one_grad + term
    keep(3, 0, 144)
    small = jnp.concatenate(
        [
            bias_grads[2],
            bias_grads[1],
            attention_bias_grad,
            *expand_bias_grads,
            contract_bias_grad,
            jnp.zeros((8, WIDE), jnp.float32),
        ],
        axis=0,
    ).astype(jnp.bfloat16)
    made[:, BIAS_ROW : BIAS_ROW + 16, :] = jnp.broadcast_to(small[None], (16, 16, WIDE))
    made[:, 592:608, :] = jnp.zeros((16, 16, WIDE), jnp.bfloat16)
    keep(4, BIAS_ROW, 16)
    keep(5, 592, 16)
    normed_one, inv_one = norm_rows(x_ref[...].astype(jnp.float32))
    terms_ref[...] = jnp.concatenate(
        [
            column_sum(mixed_one_grad),
            column_sum(mixed_one_grad * normed_one),
            gate_one_grad,
            shift_two_grad,
            scale_two_grad,
            gate_two_grad,
            jnp.zeros((2, WIDE), jnp.float32),
        ],
        axis=0,
    )
    input_grad_ref[...] += norm_back(mixed_one_grad * (1.0 + row(1)), normed_one, inv_one)
    for item in saves:
        item.wait()
    wires.finish()


def block_backward(part, gradient, tokens, modulation, blocks, kept):
    shape = lambda dims, dtype: jax.ShapeDtypeStruct(dims, dtype)
    bf, f32 = jnp.bfloat16, jnp.float32
    whole = pl.BlockSpec(memory_space=pltpu.VMEM)
    away = pl.BlockSpec(memory_space=pl.ANY)
    return pl.pallas_call(
        functools.partial(backward_kernel, part),
        out_shape=[
            shape((TOKENS, WIDE), f32),
            shape((8, WIDE), f32),
            shape((16, ROWS, WIDE), bf),
        ],
        in_specs=[whole, whole, whole, away, whole, away, whole, whole, whole, whole, whole, away, whole],
        out_specs=[whole, whole, away],
        scratch_shapes=[
            pltpu.VMEM((16, ROWS, WIDE), bf),
            pltpu.VMEM((16, ROWS, WIDE), bf),
            pltpu.VMEM((4, TOKENS, WIDE), f32),
            pltpu.VMEM((4, 3, 3, TOKENS, PAIR), bf),
            pltpu.VMEM((6, TOKENS, PAIR), bf),
            pltpu.VMEM((2, 3, TOKENS, PAIR), bf),
            pltpu.VMEM((2, 4, TOKENS, PAIR), f32),
            pltpu.VMEM((2, TOKENS, PAIR), f32),
            pltpu.VMEM((3, 3, TOKENS, PAIR), f32),
            pltpu.VMEM((3, 2, 2, TOKENS, PAIR), bf),
            pltpu.VMEM((3, 2, 2, TOKENS, PAIR), bf),
            pltpu.VMEM((3, 3, TOKENS, PAIR), bf),
            pltpu.VMEM((3, 3, TOKENS, PAIR), bf),
            pltpu.VMEM((3, 6, TOKENS, PAIR), bf),
            pltpu.SemaphoreType.DMA((4,)),
            pltpu.SemaphoreType.DMA((6,)),
            pltpu.SemaphoreType.DMA((10,)),
            pltpu.SemaphoreType.DMA((10,)),
        ],
        compiler_params=pltpu.CompilerParams(
            collective_id=4 + part, has_side_effects=True, vmem_limit_bytes=58 * 1024 * 1024
        ),
        cost_estimate=pl.CostEstimate(flops=12 * 10**9, bytes_accessed=45 * 10**6, transcendentals=4 * 10**6),
        name=("backward_first", "backward_second")[part],
    )(gradient, tokens, modulation, blocks, *kept)


def pack_weights(projection, attention, expand, contract, biases):
    fill = jnp.zeros((WIDE - biases.shape[0],), jnp.bfloat16)
    columns = lambda weight: weight.reshape(48, -1, WIDE).swapaxes(0, 1).reshape(-1, WIDE)
    return jnp.concatenate(
        [
            columns(projection),
            attention,
            columns(expand[:, : 2 * WIDE]),
            jnp.concatenate([biases, fill])[None],
            jnp.zeros((15, WIDE), jnp.bfloat16),
            columns(expand[:, 2 * WIDE :]),
            contract,
            jnp.zeros((16, WIDE), jnp.bfloat16),
        ]
    )


def bias_rows(biases):
    query_value = biases[:, :, :96].reshape(2, 2, WIDE)
    attention = biases[:, :, 96:144].reshape(2, 1, WIDE)
    expand = biases[:, :, 144:336].reshape(2, 4, WIDE)
    contract = biases[:, :, 336:384].reshape(2, 1, WIDE)
    return jnp.concatenate([query_value, attention, expand, contract], axis=1)


def unpack_grads(rows, place):
    columns = lambda part: part.reshape(-1, 48, WIDE).swapaxes(0, 1).reshape(48, -1)
    own = lambda part, size: lax.dynamic_slice_in_dim(part.reshape(-1), place * size, size)
    bias = rows[BIAS_ROW : BIAS_ROW + 8]
    return [
        columns(rows[:144]),
        own(bias[0:2], 96),
        rows[144:192],
        own(bias[2:3], 48),
        columns(jnp.concatenate([rows[192:288], rows[304:400]])),
        own(bias[3:7], 192),
        rows[400:592],
        own(bias[7:8], 48),
    ]


def on_device(
    latents,
    conditions,
    output_cotangent,
    modulation_weight,
    modulation_bias,
    projection_weight,
    projection_bias,
    attention_weight,
    attention_bias,
    expand_weight,
    expand_bias,
    contract_weight,
    contract_bias,
):
    section = lax.axis_index("section")
    place = lax.axis_index("dp")
    is_first = section == 0
    biases = jnp.concatenate(
        [projection_bias[0], attention_bias[0], expand_bias[0], contract_bias[0], modulation_bias[0]]
    )
    packed = pack_weights(projection_weight[0], attention_weight[0], expand_weight[0], contract_weight[0], biases)
    pieces = jnp.pad(conditions[:, 0].reshape(2, 16, 48).swapaxes(0, 1), ((0, 0), (0, 6), (0, PAIR - 48)))
    owned_weight = jnp.pad(modulation_weight[0], ((0, PAIR - 48), (0, 0)))
    first_blocks, second_blocks, own_conds, modulations = gather_weights(packed, pieces, owned_weight)
    biases = jnp.stack([first_blocks[:, BIAS_ROW], second_blocks[:, BIAS_ROW]]).astype(jnp.float32)
    added = jnp.pad(biases[:, :, 384:672].reshape(2, 6, WIDE), ((0, 0), (0, 2), (0, 0)))
    modulations = modulations + added
    bias = bias_rows(biases)

    tokens = lax.dynamic_index_in_dim(latents, section, 0, keepdims=False)[0]
    cotangent = lax.dynamic_index_in_dim(output_cotangent, section, 0, keepdims=False)[0]
    first_output, *first_kept = block_forward(0, tokens, modulations[0], bias[0], first_blocks)
    second_output, *second_kept = block_forward(1, first_output, modulations[1], bias[1], second_blocks)
    second_grad, second_terms, second_made = block_backward(
        1, cotangent, first_output, modulations[1], second_blocks, second_kept
    )
    second_grad = second_grad.astype(jnp.bfloat16)
    first_grad, first_terms, first_made = block_backward(0, second_grad, tokens, modulations[0], first_blocks, first_kept)

    rounded_grad = second_grad.astype(jnp.float32)
    rows, terms, cond_terms, section_outputs, input_grads = reduce_grads(
        first_made,
        second_made,
        first_terms,
        second_terms,
        owned_weight,
        jnp.where(is_first, first_output, second_output),
        jnp.where(is_first, second_output, first_output),
        jnp.where(is_first, first_grad, rounded_grad),
        jnp.where(is_first, rounded_grad, first_grad),
    )
    reduced = [grad[None] for grad in unpack_grads(rows.astype(jnp.float32), place)]
    section_outputs = section_outputs[None, :, None]
    input_grads = input_grads[None, :, None]
    terms = terms[:, :, :6].reshape(16, 2, -1)
    own_silu = jax.nn.silu(own_conds[:, :2, :48]).astype(jnp.bfloat16)
    modulation_weight_grad = jnp.einsum(
        "imk,ime->ke", own_silu, terms.astype(jnp.bfloat16), preferred_element_type=jnp.float32
    )
    modulation_bias_grad = lax.dynamic_slice_in_dim(jnp.sum(terms, axis=(0, 1)), place * 288, 288)
    cond_terms = cond_terms[:, :2, :48].swapaxes(0, 1).reshape(2, 1, WIDE)
    condition_grads = jax.vjp(jax.nn.silu, conditions)[1](cond_terms)[0]
    return (
        section_outputs,
        input_grads,
        condition_grads,
        modulation_weight_grad[None],
        modulation_bias_grad[None],
        *reduced,
    )


def solution(mesh):
    return jax.shard_map(
        on_device,
        mesh=mesh,
        in_specs=(
            P(None, "dp", "seq", None),
            P(None, "dp", None),
            P(None, "dp", "seq", None),
            P("section", "dp", None),
            P("section", "dp"),
            P("section", "dp", None),
            P("section", "dp"),
            P("section", "dp", None),
            P("section", "dp"),
            P("section", "dp", None),
            P("section", "dp"),
            P("section", "dp", None),
            P("section", "dp"),
        ),
        out_specs=(
            P("section", None, "dp", "seq", None),
            P("section", None, "dp", "seq", None),
            P(None, "dp", None),
            P("section", "dp", None),
            P("section", "dp"),
            P("section", "dp", None),
            P("section", "dp"),
            P("section", "dp", None),
            P("section", "dp"),
            P("section", "dp", None),
            P("section", "dp"),
            P("section", "dp", None),
            P("section", "dp"),
        ),
        check_vma=False,
    )
```

time: 1210 us -> 442 us (0.37)
  waiting for transfers between devices: 469 us -> 0 us
  Pallas kernels: 0 us -> 394 us
  matrix products: 230 us -> 1.22 us
  blocking collectives: 214 us -> 0 us
  other arithmetic: 99.3 us -> 9 us
  local copies, waits for them, and re-layouts: 101 us -> 29.6 us
  starting transfers between devices: 61.2 us -> 0 us
  between operations: 23.3 us -> 1.28 us
    pallas_call x0 -> x6, Pallas kernels: none -> 394 us  [the longest x1 133 us: reduce_grads(): pl.pallas_call(reduce_kernel, out_shape=[jax.ShapeDtypeStruct((ROWS, WIDE...]
    dot_general x84 -> x1, matrix products: 230 us -> 1.22 us  [on_device(): jnp.einsum('imk,ime->ke', own_silu, terms.astype(jnp.bfloat16), preferred...]
    reduce_scatter x5 -> x0, waiting for transfers between devices: 160 us -> none  [the longest x1 85.8 us: on_device(): lax.psum_scatter(grad_sums[0].astype(jnp.bfloat16), 'dp', scatter_dimensi...]
    unnamed x2 -> x0, blocking collectives: 122 us -> none
    all_gather x5 -> x0, waiting for transfers between devices: 121 us -> none  [the longest x1 50.2 us: on_device(): lax.all_gather(contract_weight[0], 'dp', axis=0, tiled=True)]
    all_to_all x9 -> x0, waiting for transfers between devices: 118 us -> none  [the longest x3 57.6 us: layer_forward(): lax.all_to_all(projected, 'seq', split_axis=3, concat_axis=1, tiled=True)]
    all_to_all x3 -> x0, blocking collectives: 50.4 us -> none  [the longest x1 28.8 us: layer_backward(): lax.all_to_all(projected_grad, 'seq', split_axis=1, concat_axis=3, tiled=...]
    all_to_all x9 -> x0, starting transfers between devices: 45.8 us -> none  [the longest x3 16.8 us: layer_forward(): lax.all_to_all(projected, 'seq', split_axis=3, concat_axis=1, tiled=True)]
  transfers between devices with their start and end apart: 24 -> 0, of which waited for: 19 -> 0; matrix products, arithmetic and copies ran while one was open for 16% -> 0% of each run, Pallas kernels for 0% -> 0%
where the time goes in v1:
time: 442 us; the launch traced here: 435 us
  Pallas kernels  394 us (89%)
  local copies, waits for them, and re-layouts  29.6 us (7%)
  other arithmetic  9 us (2%)
    pallas_call x1, Pallas kernels, reduce_grads(): pl.pallas_call(reduce_kernel, out_shape=[jax.ShapeDtypeStruct((ROWS, WIDE...  133 us
    pallas_call x1, Pallas kernels, gather_weights(): pl.pallas_call(gather_kernel, out_shape=[jax.ShapeDtypeStruct((16, ROWS,...  108 us
    pallas_call x2, Pallas kernels, block_backward(): pl.pallas_call(functools.partial(backward_kernel, part), out_shape=[shape...  86.9 us
    pallas_call x2, Pallas kernels, block_forward(): pl.pallas_call(functools.partial(forward_kernel, part), out_shape=[shape(...  65.2 us

profile of v1, /device:TPU:1, one launch (start us, length us, event | category | flops | bytes accessed | tf_op | source)
XLA Modules:
  0.0 435.0 jit_solution(12874371154995740129)
XLA Ops:
  0.7 0.8 reduce.1
  1.5 0.7 reduce.2
  2.2 2.1 concatenate.12
  4.3 0.7 reduce.3
  5.1 1.0 reshape_squeeze.6
  6.2 1.1 fusion.7
  7.9 1.9 dynamic-slice_bitcast_fusion
  9.9 108.4 %gather_weights.1 = (bf16[16,608,768]{2,1,0:T(8,128)(2,1)S(1)}, bf16[16,608,768]{2,1,0:T(8,128)(2,1)}, f32[16,8,128]{2,1,0:T(8,128)S(1)}, f32[2,8,768]{2,1,0:T(8,128)S(1)}) custom-call(bf16[608,768]{1,0:T(8,128)(2,1)S(1)} %concatenate.13.p_ref, f32[16,8,128]{2,1,0:T(8,128)S(1)} %pad.12.conds_ref, bf16[128,4608]{1,0:T(8,128)(2,1)S(1)} %pad.13.weight_ref), custom_call_target="tpu_custom_call" | custom-call | bytes 60000000 | tf_op jit(solution)/shard_map/gather_weights/pallas_call | solution.py:338
  118.4 5.2 %copy-done.1 = bf16[16,608,768]{2,1,0:T(8,128)(2,1)} copy-done((bf16[16,608,768]{2,1,0:T(8,128)(2,1)}, bf16[16,608,768]{2,1,0:T(8,128)(2,1)S(1)}, u32[]{:S(2)}) %copy-start.1) | copy-done | bytes 14942232
  123.6 1.0 slice.85
  126.5 32.0 %forward_first.1 = (bf16[256,768]{1,0:T(8,128)(2,1)}, bf16[256,768]{1,0:T(8,128)(2,1)}, bf16[4,3,3,256,128]{4,3,2,1,0:T(8,128)(2,1)}, f32[12,1,256]{2,1,0:T(1,12...) custom-call(bf16[256,768]{1,0:T(8,128)(2,1)} %get-tuple-element.151., ...), custom_call_target="tpu_custom_call" | custom-call | flops 5000000000 | bytes 25000000 | tf_op jit(solution)/shard_map/forward_first/pallas_call | solution.py:736
  158.5 33.3 %forward_second.1 = (bf16[256,768]{1,0:T(8,128)(2,1)}, bf16[256,768]{1,0:T(8,128)(2,1)}, bf16[4,3,3,256,128]{4,3,2,1,0:T(8,128)(2,1)}, f32[12,1,256]{2,1,0:T(1,1...) custom-call(bf16[256,768]{1,0:T(8,128)(2,1)} %get-tuple-element.51.x, ...), custom_call_target="tpu_custom_call" | custom-call | flops 5000000000 | bytes 25000000 | tf_op jit(solution)/shard_map/forward_second/pallas_call | solution.py:736
  191.8 44.4 %backward_second.1 = (f32[256,768]{1,0:T(8,128)}, f32[8,768]{1,0:T(8,128)}, bf16[16,608,768]{2,1,0:T(8,128)(2,1)}) custom-call(bf16[256,768]{1,0:T(8,128)(2,1)} %get-tuple-element.152.grad_ref, bf16[256,768]{1,0:T(8,128)(2,1)} %get-tuple-element.51.x_ref, f32[8,768]{1,0:T(8,128)} %get-tuple-element.147.mod_ref, ...), custom_call_target="tpu_custom_call" | custom-call | flops 12000000000 | bytes 45000000 | tf_op jit(solution)/shard_map/backward_second/pallas_call | solution.py:939
  236.2 0.9 broadcast_select_fusion
  237.2 1.9 convert_element_type.28.grad_ref
  239.1 42.5 %backward_first.1 = (f32[256,768]{1,0:T(8,128)}, f32[8,768]{1,0:T(8,128)}, bf16[16,608,768]{2,1,0:T(8,128)(2,1)}) custom-call(bf16[256,768]{1,0:T(8,128)(2,1)} %convert_element_type.28.grad_ref, bf16[256,768]{1,0:T(8,128)(2,1)} %get-tuple-element.151.x_ref, f32[8,768]{1,0:T(8,128)} %get-tuple-element.148.mod_ref, bf16[16,608,768]{2,1,0:T(8,128)(2,1)} %copy-done.1, ...), custom_call_target="tpu_custom_call" | custom-call | flops 12000000000 | bytes 45000000 | tf_op jit(solution)/shard_map/backward_first/pallas_call | solution.py:939
  281.6 2.4 convert_select_fusion
  284.0 133.4 %reduce_grads.1 = (bf16[608,768]{1,0:T(8,128)(2,1)}, f32[16,2,8,768]{3,2,1,0:T(8,128)}, f32[16,8,128]{2,1,0:T(8,128)}, bf16[2,256,768]{2,1,0:T(8,128)(2,1)}, f32[2,256,768]{2,1,0:T(8,128)}) custom-call(bf16[16,608,768]{2,1,0:T(8,128)(2,1)} %get-tuple-element.71.first_ref, bf16[16,608,768]{2,1,0:T(8,128)(2,1)} %get-tuple-element.72.second_ref, ...), custom_call_target="tpu_custom_call" | custom-call | bytes 60000000 | tf_op jit(solution)/shard_map/reduce_grads/pallas_call | solution.py:585
  417.3 0.8 slice.116
  418.7 0.8 fusion.5
  420.7 0.7 slice.121
  421.4 0.6 dynamic_slice.27
  422.1 0.8 slice_bitcast_fusion.6
  423.6 1.2 slice_reduce_fusion
  424.8 1.2 slice.136
  427.2 1.1 broadcast_in_dim_reshape.6
  428.3 1.2 convolution_bitcast_fusion
  430.0 1.1 broadcast_in_dim_reshape.7
  431.2 0.7 slice_bitcast_fusion.1
  431.9 0.9 slice_bitcast_fusion
  432.7 0.9 copy.102
  433.6 1.1 copy.103
  (73 shorter events, 7.0 us)
Async XLA Ops:
  0.6 6.7 %copy-start.9 = (bf16[1,192,768]{2,1,0:T(8,128)(2,1)S(1)}, bf16[1,192,768]{2,1,0:T(8,128)(2,1)}, u32[]{:S(2)}) copy-start(bf16[1,192,768]{2,1,0:T(8,128)(2,1)} %param.24) | copy-start | bytes 884740
  0.7 6.7 %copy-start.11 = (bf16[1,48,768]{2,1,0:T(8,128)(2,1)S(1)}, bf16[1,48,768]{2,1,0:T(8,128)(2,1)}, u32[]{:S(2)}) copy-start(bf16[1,48,768]{2,1,0:T(8,128)(2,1)} %param.20) | copy-start | bytes 221188
  0.7 7.2 %copy-start.10 = (bf16[2,1,256,768]{3,2,1,0:T(8,128)(2,1)S(1)}, bf16[2,1,256,768]{3,2,1,0:T(8,128)(2,1)}, u32[]{:S(2)}) copy-start(bf16[2,1,256,768]{3,2,1,0:T(8,128)(2,1)} %param.13) | copy-start | bytes 2359300
  6.2 3.6 copy-start.6
  9.9 148.6 %copy-start = (bf16[128,4608]{1,0:T(8,128)(2,1)}, bf16[128,4608]{1,0:T(8,128)(2,1)S(1)}, u32[]{:S(2)}) copy-start(bf16[128,4608]{1,0:T(8,128)(2,1)S(1)} %pad.13.weight_ref) | copy-start | bytes 3538948
  118.3 5.3 %copy-start.1 = (bf16[16,608,768]{2,1,0:T(8,128)(2,1)}, bf16[16,608,768]{2,1,0:T(8,128)(2,1)S(1)}, u32[]{:S(2)}) copy-start(bf16[16,608,768]{2,1,0:T(8,128)(2,1)S(1)} %get-tuple-element.49.w_hbm) | copy-start | bytes 44826628
  191.8 44.4 %copy-start.7 = (bf16[256,768]{1,0:T(8,128)(2,1)S(1)}, bf16[256,768]{1,0:T(8,128)(2,1)}, u32[]{:S(2)}) copy-start(bf16[256,768]{1,0:T(8,128)(2,1)} %get-tuple-element.51.x_ref) | copy-start | bytes 1179652
  191.8 44.4 %copy-start.8 = (bf16[256,768]{1,0:T(8,128)(2,1)S(1)}, bf16[256,768]{1,0:T(8,128)(2,1)}, u32[]{:S(2)}) copy-start(bf16[256,768]{1,0:T(8,128)(2,1)} %get-tuple-element.75) | copy-start | bytes 1179652
  239.1 42.5 %copy-start.3 = (f32[256,768]{1,0:T(8,128)S(1)}, f32[256,768]{1,0:T(8,128)}, u32[]{:S(2)}) copy-start(f32[256,768]{1,0:T(8,128)} %get-tuple-element.61) | copy-start | bytes 2359300
  283.9 139.0 %copy-start.12 = (f32[2,1,768]{2,1,0:T(1,128)S(1)}, f32[2,1,768]{2,1,0:T(1,128)}, u32[]{:S(2)}) copy-start(f32[2,1,768]{2,1,0:T(1,128)} %param.14) | copy-start | bytes 18436
  417.3 9.5 %copy-start.2 = (bf16[608,768]{1,0:T(8,128)(2,1)S(1)}, bf16[608,768]{1,0:T(8,128)(2,1)}, u32[]{:S(2)}) copy-start(bf16[608,768]{1,0:T(8,128)(2,1)} %get-tuple-element.82) | copy-start | bytes 2801668
  431.1 1.7 copy-start.5
  431.1 2.5 copy-start.4

commit v2 on v1

--- a/solution.py
+++ b/solution.py
@@ -300,7 +300,7 @@
     return [swap[0], swap[1], multiply, add_b, add_a, end]
 
 
-def gather_kernel(p_ref, conds_ref, weight_ref, first_ref, second_ref, columns_ref, mod_ref, shard, c_first, c_second, partial, b_sums, a_sums, across_sums, local, send, recv):
+def gather_kernel(p_ref, conds_ref, weight_ref, first_ref, shard_out, columns_ref, mod_ref, shard, c_first, c_second, partial, b_sums, a_sums, across_sums, local, send, recv):
     me = Place()
     mine = p_ref.at[half_rows(me.c, 0, HALF), :]
     own = pltpu.make_async_copy(mine, shard.at[me.s], local.at[2])
@@ -308,25 +308,28 @@
     greet(me.grid_peers() + [me.across(), me.flipped(), me.sibling()])
     wires = Wires(send, recv)
     wires.push(0, mine, shard.at[me.s], me.across())
-    small = modulation_steps(me, wires, 73, conds_ref, weight_ref, columns_ref, mod_ref, c_first, c_second, partial, b_sums, a_sums, across_sums)
+    small = modulation_steps(me, wires, 37, conds_ref, weight_ref, columns_ref, mod_ref, c_first, c_second, partial, b_sums, a_sums, across_sums)
     small[0]()
     small[1]()
     own.wait()
     wires.got(0, shard.at[1 - me.s], me.across())
+    handed = pltpu.make_async_copy(shard.at[1], shard_out, local.at[1])
+    handed.start()
     one = gather_steps(me, wires, 1, shard.at[0], first_ref, local.at[0])
-    two = gather_steps(me, wires, 37, shard.at[1], second_ref, local.at[1])
     one[0]()
-    two[0]()
     small[2]()
     one[1]()
+    one[2]()
     small[3]()
-    one[2]()
-    two[1]()
+    one[3]()
+    one[4]()
     small[4]()
-    two[2]()
+    one[5]()
+    one[6]()
     small[5]()
-    for step in one[3:7] + two[3:7] + one[7:11] + two[7:11] + [one[11], two[11]]:
+    for step in one[7:]:
         step()
+    handed.wait()
     wires.finish()
 
 
@@ -339,7 +342,7 @@
         gather_kernel,
         out_shape=[
             jax.ShapeDtypeStruct((16, ROWS, WIDE), bf),
-            jax.ShapeDtypeStruct((16, ROWS, WIDE), bf),
+            jax.ShapeDtypeStruct((HALF, WIDE), bf),
             jax.ShapeDtypeStruct((16, 8, PAIR), f32),
             jax.ShapeDtypeStruct((2, 8, WIDE), f32),
         ],
@@ -354,8 +357,8 @@
             pltpu.VMEM((4, 8, wide), f32),
             pltpu.VMEM((2, 8, wide), f32),
             pltpu.SemaphoreType.DMA((3,)),
-            pltpu.SemaphoreType.DMA((86,)),
-            pltpu.SemaphoreType.DMA((86,)),
+            pltpu.SemaphoreType.DMA((50,)),
+            pltpu.SemaphoreType.DMA((50,)),
         ],
         compiler_params=pltpu.CompilerParams(
             collective_id=0, has_side_effects=True, vmem_limit_bytes=24 * 1024 * 1024
@@ -521,22 +524,21 @@
 
 
 def reduce_kernel(
-    first_ref, second_ref, first_terms, second_terms, weight_ref, kept_out, sent_out, kept_grad, sent_grad,
+    first_ref, second_rows, first_terms, second_terms, weight_ref, kept_out, sent_out, kept_grad, sent_grad,
     o_ref, all_ref, conds_ref, outs_ref, grads_ref,
-    mine, sib, r_top, r_low, r_left, r_right, a_top, a_low, a_left, a_right, r_across, r_beside,
+    mine, sib, r_top, r_low, r_left, r_right, a_top, a_low, a_left, a_right, final, r_across, r_beside,
     sums, rounded, tiles, c_first, c_second, load, local, send, recv,
 ):
     me = Place()
     greet(me.grid_peers() + [me.across(), me.flipped(), me.beside(), me.askew(), me.sibling()])
     wires = Wires(send, recv)
     buffers = (mine, sib, r_top, r_low, r_left, r_right, a_top, a_low, a_left, a_right)
-    one = reduce_steps(me, wires, 0, second_ref, load.at[1], [ref.at[1] for ref in buffers])
-    two = reduce_steps(me, wires, 36, first_ref, load.at[0], [ref.at[0] for ref in buffers])
+    two = reduce_steps(me, wires, 36, first_ref, load, buffers)
     small = terms_steps(me, wires, 77, first_terms, second_terms, weight_ref, all_ref, conds_ref, sums, rounded, tiles, c_first, c_second)
-    one[0]()
     two[0]()
     small[0]()
     keeps = [
+        pltpu.make_async_copy(second_rows, final.at[1], local.at[3]),
         pltpu.make_async_copy(kept_out, outs_ref.at[me.s], local.at[0]),
         pltpu.make_async_copy(kept_grad, grads_ref.at[me.s], local.at[1]),
     ]
@@ -544,16 +546,19 @@
         item.start()
     wires.push(72, sent_out, outs_ref.at[me.s], me.flipped())
     wires.push(73, sent_grad, grads_ref.at[me.s], me.flipped())
-    big = one[1:5] + two[1:5] + one[5:9] + two[5:9] + one[9:13] + two[9:13] + [one[13], two[13], one[14], two[14]]
+    big = two[1:]
     small = small[1:]
     for index, step in enumerate(big):
         step()
-        if index % 3 == 2 and small:
+        if index % 2 == 1 and small:
             small.pop(0)()
     while small:
         small.pop(0)()
-    held = mine.at[me.s, me.d]
-    wires.push(74, mine.at[1 - me.s, me.d], r_across, me.across())
+    final[0] = mine[me.d]
+    for item in keeps:
+        item.wait()
+    held = final.at[me.s]
+    wires.push(74, final.at[1 - me.s], r_across, me.across())
     wires.got(74, r_across, me.across())
     add_rows(held, [(r_across, 0)])
     beside = pltpu.make_async_remote_copy(
@@ -568,12 +573,26 @@
     own = pltpu.make_async_copy(held, out_rows, local.at[2])
     own.start()
     own.wait()
-    for item in keeps:
-        item.wait()
     wires.got(72, outs_ref.at[1 - me.s], me.flipped())
     wires.got(73, grads_ref.at[1 - me.s], me.flipped())
     wires.got(76, o_ref.at[half_rows(1 - me.c, 0, HALF), :], me.sibling())
     wires.finish()
+
+
+def reduce_buffers():
+    blocks = lambda *lead: pltpu.VMEM(lead + (WIDE,), jnp.bfloat16)
+    return [
+        blocks(16, HALF),
+        blocks(16, HALF),
+        blocks(4, TOP),
+        blocks(4, LOW),
+        blocks(4, HALF),
+        blocks(4, HALF),
+        blocks(TOP),
+        blocks(LOW),
+        blocks(HALF),
+        blocks(HALF),
+    ]
 
 
 def reduce_grads(*operands):
@@ -594,15 +613,7 @@
         in_specs=[away, away, whole, whole, whole, away, away, away, away],
         out_specs=[away, whole, whole, away, away],
         scratch_shapes=[
-            blocks(2, 16, HALF),
-            blocks(2, 16, HALF),
-            blocks(2, 4, TOP),
-            blocks(2, 4, LOW),
-            blocks(2, 4, HALF),
-            blocks(2, 4, HALF),
-            blocks(2, TOP),
-            blocks(2, LOW),
-            blocks(2, HALF),
+            *reduce_buffers(),
             blocks(2, HALF),
             blocks(HALF),
             blocks(HALF),
@@ -611,13 +622,13 @@
             pltpu.VMEM((3, 16, 8, PAIR), f32),
             pltpu.VMEM((2, 4, 4, 8, PAIR), f32),
             pltpu.VMEM((2, 4, 4, 8, PAIR), f32),
-            pltpu.SemaphoreType.DMA((2, 16)),
-            pltpu.SemaphoreType.DMA((3,)),
+            pltpu.SemaphoreType.DMA((16,)),
+            pltpu.SemaphoreType.DMA((4,)),
             pltpu.SemaphoreType.DMA((count,)),
             pltpu.SemaphoreType.DMA((count,)),
         ],
         compiler_params=pltpu.CompilerParams(
-            collective_id=1, has_side_effects=True, vmem_limit_bytes=57 * 1024 * 1024
+            collective_id=1, has_side_effects=True, vmem_limit_bytes=48 * 1024 * 1024
         ),
         cost_estimate=pl.CostEstimate(flops=0, bytes_accessed=60000000, transcendentals=0),
         name="reduce_grads",
@@ -630,18 +641,28 @@
 
 
 def forward_kernel(
-    part, x_ref, mod_ref, bias_ref, w_hbm,
-    out_ref, mixed_one_ref, qkv_out, lse_ref, att_out, branch_one_ref, middle_ref, mixed_two_ref, expanded_out, branch_two_ref,
-    w, stage, qkv, heads, att, expanded, load, save, send, recv,
+    part, x_ref, mod_ref, bias_ref, w_hbm, *refs
 ):
+    shard_ref, refs = (refs[0], refs[1:]) if part == 0 else (None, refs)
+    out_ref, mixed_one_ref, qkv_out, lse_ref, att_out, branch_one_ref, middle_ref, mixed_two_ref, expanded_out, branch_two_ref, *refs = refs
+    next_ref, refs = (refs[0], refs[1:]) if part == 0 else (None, refs)
+    w, stage, qkv, heads, att, expanded, load, save, send, recv = refs
     me = Place()
     sibling, far = seq_peers(me)
     first_load = pltpu.make_async_copy(w_hbm.at[:, pl.ds(0, 144), :], w.at[:, pl.ds(0, 144), :], load.at[0])
     rest_load = pltpu.make_async_copy(w_hbm.at[:, pl.ds(144, 464), :], w.at[:, pl.ds(144, 464), :], load.at[1])
     first_load.start()
     rest_load.start()
-    greet([sibling, *far])
+    around = [me.ring(1, 0), me.ring(3, 0), me.ring(0, 1), me.ring(0, 3)] if part == 0 else []
+    greet([sibling, *far, *around])
     wires = Wires(send, recv)
+    beside = gather_steps(me, wires, 12, shard_ref, next_ref, load.at[2]) if part == 0 else []
+
+    def advance(count):
+        for _ in range(min(count, len(beside))):
+            beside.pop(0)()
+
+    advance(1)
 
     row = lambda index: mod_ref[index : index + 1, :]
     bias = lambda index: bias_ref[index : index + 1, :]
@@ -665,11 +686,13 @@
         for g in range(2):
             wires.push(2 * j + g, stage.at[3 * g + j, pl.ds(0, 2)], qkv.at[2 + me.c, j, pl.ds(0, 2)], far[g], 2 * j + me.c)
     project(2, 0, bias(0))
+    advance(1)
     for j in range(3):
         wires.push(6 + j, stage.at[3 * (1 - me.c) + j], qkv.at[me.c, j], sibling)
     for j in range(3):
         qkv[me.c, j] = stage[3 * me.c + j]
 
+    advance(1)
     for j in range(3):
         wires.got(6 + j, qkv.at[1 - me.c, j], sibling)
         for g in range(2):
@@ -694,6 +717,7 @@
         lax.fori_loop(0, 2, queries_step, 0)
         wires.push(9 + j, heads.at[1 - me.c, j], att.at[3 * me.c + j], sibling)
         att[3 * me.c + j] = heads[me.c, j]
+        advance(1)
     qkv_save = pltpu.make_async_copy(qkv, qkv_out, save.at[0])
     qkv_save.start()
     rest_load.wait()
@@ -704,6 +728,7 @@
     attended = side_by_side(att)
     branch_one = dot(attended, square(w, 144)) + bias(2)
     branch_one_ref[...] = branch_one
+    advance(1)
     middle = tokens + row(2) * branch_one
     middle_ref[...] = middle
     normed_two, _ = norm_rows(middle)
@@ -719,8 +744,10 @@
         saves.append(item)
         activated = (0.5 * u * (1.0 + jnp.tanh(ROOT * (u + 0.044715 * (u * u * u))))).astype(jnp.bfloat16)
         total = total + dot(activated, contract_square(w, k))
+        advance(1)
     branch_two_ref[...] = total
     out_ref[...] = (middle + row(5) * total).astype(jnp.bfloat16)
+    advance(12)
     qkv_save.wait()
     att_save.wait()
     for item in saves:
@@ -728,7 +755,7 @@
     wires.finish()
 
 
-def block_forward(part, tokens, modulation, bias, blocks):
+def block_forward(part, tokens, modulation, bias, blocks, *shard):
     shape = lambda dims, dtype: jax.ShapeDtypeStruct(dims, dtype)
     bf, f32 = jnp.bfloat16, jnp.float32
     whole = pl.BlockSpec(memory_space=pltpu.VMEM)
@@ -746,9 +773,10 @@
             shape((TOKENS, WIDE), bf),
             shape((4, TOKENS, WIDE), f32),
             shape((TOKENS, WIDE), f32),
-        ],
-        in_specs=[whole, whole, whole, away],
-        out_specs=[whole, whole, away, whole, away, whole, whole, whole, away, whole],
+        ]
+        + [shape((16, ROWS, WIDE), bf) for _ in shard],
+        in_specs=[whole, whole, whole, away] + [away for _ in shard],
+        out_specs=[whole, whole, away, whole, away, whole, whole, whole, away, whole] + [away for _ in shard],
         scratch_shapes=[
             pltpu.VMEM((16, ROWS, WIDE), bf),
             pltpu.VMEM((6, 3, TOKENS, PAIR), bf),
@@ -756,24 +784,26 @@
             pltpu.VMEM((2, 3, TOKENS, PAIR), bf),
             pltpu.VMEM((6, TOKENS, PAIR), bf),
             pltpu.VMEM((4, TOKENS, WIDE), f32),
-            pltpu.SemaphoreType.DMA((2,)),
+            pltpu.SemaphoreType.DMA((3,)),
             pltpu.SemaphoreType.DMA((6,)),
-            pltpu.SemaphoreType.DMA((12,)),
-            pltpu.SemaphoreType.DMA((12,)),
+            pltpu.SemaphoreType.DMA((48,)),
+            pltpu.SemaphoreType.DMA((48,)),
         ],
         compiler_params=pltpu.CompilerParams(
             collective_id=2 + part, has_side_effects=True, vmem_limit_bytes=56 * 1024 * 1024
         ),
         cost_estimate=pl.CostEstimate(flops=5 * 10**9, bytes_accessed=25 * 10**6, transcendentals=4 * 10**6),
         name=("forward_first", "forward_second")[part],
-    )(tokens, modulation, bias, blocks)
+    )(tokens, modulation, bias, blocks, *shard)
 
 
 def backward_kernel(
-    part, grad_ref, x_ref, mod_ref, w_hbm, mixed_one_ref, qkv_in, lse_ref, att_ref, branch_one_ref, middle_ref, mixed_two_ref, expanded_in, branch_two_ref,
-    input_grad_ref, terms_ref, grads_out,
-    w, made, expanded, qkv, stage, given, dkv, dq, own, far_out, far_in, side_out, side_in, joined, load, save, send, recv,
+    part, grad_ref, x_ref, mod_ref, w_hbm, mixed_one_ref, qkv_in, lse_ref, att_ref, branch_one_ref, middle_ref, mixed_two_ref, expanded_in, branch_two_ref, *refs
 ):
+    later_ref, refs = (refs[0], refs[1:]) if part == 0 else (None, refs)
+    input_grad_ref, terms_ref, grads_out, *refs = refs
+    rows_out, refs = (refs[0], refs[1:]) if part == 0 else (None, refs)
+    w, expanded, qkv, stage, given, dkv, dq, own, far_out, far_in, side_out, side_in, joined, load, save, send, recv, *refs = refs
     me = Place()
     sibling, far = seq_peers(me)
     c, other = me.c, 1 - me.c
@@ -785,13 +815,21 @@
     expanded_load.start()
     front_load.start()
     qkv_load.start()
-    greet([sibling, *far])
+    around = [me.ring(1, 0), me.ring(3, 0), me.ring(0, 1), me.ring(0, 3)] if part == 0 else []
+    greet([sibling, *far, *around])
     wires = Wires(send, recv)
+    beside = reduce_steps(me, wires, 10, later_ref, refs[-1], refs[:-1]) if part == 0 else []
+
+    def advance(count):
+        for _ in range(min(count, len(beside))):
+            beside.pop(0)()
+
+    advance(1)
     saves = []
 
     def keep(index, start, count):
         rows = pl.ds(start, count)
-        item = pltpu.make_async_copy(made.at[:, rows, :], grads_out.at[:, rows, :], save.at[index])
+        item = pltpu.make_async_copy(w.at[:, rows, :], grads_out.at[:, rows, :], save.at[index])
         item.start()
         saves.append(item)
 
@@ -812,15 +850,16 @@
         half = 0.5 * (1.0 + tanh)
         activated = (u * half).astype(jnp.bfloat16)
         slope = half + 0.5 * u * (1.0 - tanh * tanh) * (ROOT * (1.0 + (3.0 * 0.044715) * squared))
-        made[4 * k : 4 * k + 4, CONTRACT_ROW : CONTRACT_ROW + 192, :] = (
-            dot(activated, branch_two_grad, 0, 0).astype(jnp.bfloat16).reshape(4, 192, WIDE)
-        )
         expanded_grad = (dot(branch_two_grad, contract_square(w, k), 1, 1) * slope).astype(jnp.bfloat16)
         start = EXPAND_ROWS[k]
-        made[:, start : start + 48, :] = dot(mixed_two, expanded_grad, 0, 0).astype(jnp.bfloat16).reshape(16, 48, WIDE)
         expand_bias_grads.append(column_sum(expanded_grad))
         term = dot(expanded_grad, square(w, start), 1, 1)
         mixed_two_grad = term if mixed_two_grad is None else mixed_two_grad + term
+        w[4 * k : 4 * k + 4, CONTRACT_ROW : CONTRACT_ROW + 192, :] = (
+            dot(activated, branch_two_grad, 0, 0).astype(jnp.bfloat16).reshape(4, 192, WIDE)
+        )
+        w[:, start : start + 48, :] = dot(mixed_two, expanded_grad, 0, 0).astype(jnp.bfloat16).reshape(16, 48, WIDE)
+        advance(1)
     keep(0, 304, 288)
     keep(1, 192, 96)
     normed_two, inv_two = norm_rows(middle_ref[...])
@@ -834,11 +873,13 @@
     for pair in range(6):
         stage[pair] = attended_grad[:, pair * PAIR : (pair + 1) * PAIR]
     wires.push(0, stage.at[pl.ds(3 * other, 3)], given.at[c], sibling)
+    advance(1)
     given[c] = stage[pl.ds(3 * c, 3)]
     input_grad_ref[...] = middle_grad
-    made[:, 144:192, :] = dot(side_by_side(att_ref), branch_one_grad, 0, 0).astype(jnp.bfloat16).reshape(16, 48, WIDE)
+    w[:, 144:192, :] = dot(side_by_side(att_ref), branch_one_grad, 0, 0).astype(jnp.bfloat16).reshape(16, 48, WIDE)
     keep(2, 144, 48)
     attention_bias_grad = column_sum(branch_one_grad)
+    advance(1)
     qkv_load.wait()
     wires.got(0, given.at[other], sibling)
 
@@ -876,6 +917,7 @@
         wires.push(7 + j, side_out.at[j], side_in.at[j], sibling)
         own[j, 0:2] = dkv[:, c]
         own[j, 2] = dq[c]
+        advance(1 if j == 0 else 2)
 
     for j in range(3):
         wires.got(7 + j, side_in.at[j], sibling)
@@ -893,9 +935,10 @@
     for kind, start in ((0, 48), (1, 96), (2, 0)):
         piece = side_by_side(joined, (kind,))
         bias_grads.append(column_sum(piece))
-        made[:, start : start + 48, :] = dot(mixed_one, piece, 0, 0).astype(jnp.bfloat16).reshape(16, 48, WIDE)
         term = dot(piece, square(w, start), 1, 1)
         mixed_one_grad = term if mixed_one_grad is None else mixed_one_grad + term
+        w[:, start : start + 48, :] = dot(mixed_one, piece, 0, 0).astype(jnp.bfloat16).reshape(16, 48, WIDE)
+        advance(1)
     keep(3, 0, 144)
     small = jnp.concatenate(
         [
@@ -908,8 +951,8 @@
         ],
         axis=0,
     ).astype(jnp.bfloat16)
-    made[:, BIAS_ROW : BIAS_ROW + 16, :] = jnp.broadcast_to(small[None], (16, 16, WIDE))
-    made[:, 592:608, :] = jnp.zeros((16, 16, WIDE), jnp.bfloat16)
+    w[:, BIAS_ROW : BIAS_ROW + 16, :] = jnp.broadcast_to(small[None], (16, 16, WIDE))
+    w[:, 592:608, :] = jnp.zeros((16, 16, WIDE), jnp.bfloat16)
     keep(4, BIAS_ROW, 16)
     keep(5, 592, 16)
     normed_one, inv_one = norm_rows(x_ref[...].astype(jnp.float32))
@@ -926,12 +969,17 @@
         axis=0,
     )
     input_grad_ref[...] += norm_back(mixed_one_grad * (1.0 + row(1)), normed_one, inv_one)
+    advance(16)
+    if part == 0:
+        rows_save = pltpu.make_async_copy(refs[0].at[me.d], rows_out, load.at[0])
+        rows_save.start()
+        rows_save.wait()
     for item in saves:
         item.wait()
     wires.finish()
 
 
-def block_backward(part, gradient, tokens, modulation, blocks, kept):
+def block_backward(part, gradient, tokens, modulation, blocks, kept, *later):
     shape = lambda dims, dtype: jax.ShapeDtypeStruct(dims, dtype)
     bf, f32 = jnp.bfloat16, jnp.float32
     whole = pl.BlockSpec(memory_space=pltpu.VMEM)
@@ -942,11 +990,11 @@
             shape((TOKENS, WIDE), f32),
             shape((8, WIDE), f32),
             shape((16, ROWS, WIDE), bf),
-        ],
-        in_specs=[whole, whole, whole, away, whole, away, whole, whole, whole, whole, whole, away, whole],
-        out_specs=[whole, whole, away],
+        ]
+        + [shape((HALF, WIDE), bf) for _ in later],
+        in_specs=[whole, whole, whole, away, whole, away, whole, whole, whole, whole, whole, away, whole] + [away for _ in later],
+        out_specs=[whole, whole, away] + [away for _ in later],
         scratch_shapes=[
-            pltpu.VMEM((16, ROWS, WIDE), bf),
             pltpu.VMEM((16, ROWS, WIDE), bf),
             pltpu.VMEM((4, TOKENS, WIDE), f32),
             pltpu.VMEM((4, 3, 3, TOKENS, PAIR), bf),
@@ -962,15 +1010,16 @@
             pltpu.VMEM((3, 6, TOKENS, PAIR), bf),
             pltpu.SemaphoreType.DMA((4,)),
             pltpu.SemaphoreType.DMA((6,)),
-            pltpu.SemaphoreType.DMA((10,)),
-            pltpu.SemaphoreType.DMA((10,)),
-        ],
+            pltpu.SemaphoreType.DMA((46,)),
+            pltpu.SemaphoreType.DMA((46,)),
+        ]
+        + ([*reduce_buffers(), pltpu.SemaphoreType.DMA((16,))] if later else []),
         compiler_params=pltpu.CompilerParams(
-            collective_id=4 + part, has_side_effects=True, vmem_limit_bytes=58 * 1024 * 1024
+            collective_id=4 + part, has_side_effects=True, vmem_limit_bytes=60 * 1024 * 1024
         ),
         cost_estimate=pl.CostEstimate(flops=12 * 10**9, bytes_accessed=45 * 10**6, transcendentals=4 * 10**6),
         name=("backward_first", "backward_second")[part],
-    )(gradient, tokens, modulation, blocks, *kept)
+    )(gradient, tokens, modulation, blocks, *kept, *later)
 
 
 def pack_weights(projection, attention, expand, contract, biases):
@@ -991,11 +1040,14 @@
 
 
 def bias_rows(biases):
-    query_value = biases[:, :, :96].reshape(2, 2, WIDE)
-    attention = biases[:, :, 96:144].reshape(2, 1, WIDE)
-    expand = biases[:, :, 144:336].reshape(2, 4, WIDE)
-    contract = biases[:, :, 336:384].reshape(2, 1, WIDE)
-    return jnp.concatenate([query_value, attention, expand, contract], axis=1)
+    parts = [
+        biases[:, :96].reshape(2, WIDE),
+        biases[:, 96:144].reshape(1, WIDE),
+        biases[:, 144:336].reshape(4, WIDE),
+        biases[:, 336:384].reshape(1, WIDE),
+    ]
+    added = jnp.pad(biases[:, 384:672].reshape(6, WIDE), ((0, 2), (0, 0)))
+    return jnp.concatenate(parts), added
 
 
 def unpack_grads(rows, place):
@@ -1038,26 +1090,28 @@
     packed = pack_weights(projection_weight[0], attention_weight[0], expand_weight[0], contract_weight[0], biases)
     pieces = jnp.pad(conditions[:, 0].reshape(2, 16, 48).swapaxes(0, 1), ((0, 0), (0, 6), (0, PAIR - 48)))
     owned_weight = jnp.pad(modulation_weight[0], ((0, PAIR - 48), (0, 0)))
-    first_blocks, second_blocks, own_conds, modulations = gather_weights(packed, pieces, owned_weight)
-    biases = jnp.stack([first_blocks[:, BIAS_ROW], second_blocks[:, BIAS_ROW]]).astype(jnp.float32)
-    added = jnp.pad(biases[:, :, 384:672].reshape(2, 6, WIDE), ((0, 0), (0, 2), (0, 0)))
-    modulations = modulations + added
-    bias = bias_rows(biases)
+    first_blocks, shard, own_conds, modulations = gather_weights(packed, pieces, owned_weight)
+    first_bias, first_added = bias_rows(first_blocks[:, BIAS_ROW].astype(jnp.float32))
+    first_modulation = modulations[0] + first_added
 
     tokens = lax.dynamic_index_in_dim(latents, section, 0, keepdims=False)[0]
     cotangent = lax.dynamic_index_in_dim(output_cotangent, section, 0, keepdims=False)[0]
-    first_output, *first_kept = block_forward(0, tokens, modulations[0], bias[0], first_blocks)
-    second_output, *second_kept = block_forward(1, first_output, modulations[1], bias[1], second_blocks)
+    first_output, *first_kept, second_blocks = block_forward(0, tokens, first_modulation, first_bias, first_blocks, shard)
+    second_bias, second_added = bias_rows(second_blocks[:, BIAS_ROW].astype(jnp.float32))
+    second_modulation = modulations[1] + second_added
+    second_output, *second_kept = block_forward(1, first_output, second_modulation, second_bias, second_blocks)
     second_grad, second_terms, second_made = block_backward(
-        1, cotangent, first_output, modulations[1], second_blocks, second_kept
+        1, cotangent, first_output, second_modulation, second_blocks, second_kept
     )
     second_grad = second_grad.astype(jnp.bfloat16)
-    first_grad, first_terms, first_made = block_backward(0, second_grad, tokens, modulations[0], first_blocks, first_kept)
+    first_grad, first_terms, first_made, second_rows = block_backward(
+        0, second_grad, tokens, first_modulation, first_blocks, first_kept, second_made
+    )
 
     rounded_grad = second_grad.astype(jnp.float32)
     rows, terms, cond_terms, section_outputs, input_grads = reduce_grads(
         first_made,
-        second_made,
+        second_rows,
         first_terms,
         second_terms,
         owned_weight,

time: 442 us -> 404 us (0.914)
  Pallas kernels: 394 us -> 357 us
    pallas_call x1, Pallas kernels: 108 us -> 70 us  [gather_weights(): pl.pallas_call(gather_kernel, out_shape=[jax.ShapeDtypeStruct((16, ROWS,...]
    pallas_call x1, Pallas kernels: 133 us -> 101 us  [reduce_grads(): pl.pallas_call(reduce_kernel, out_shape=[jax.ShapeDtypeStruct((ROWS, WIDE...]
    pallas_call x2, Pallas kernels: 86.9 us -> 104 us  [block_backward(): pl.pallas_call(functools.partial(backward_kernel, part), out_shape=[shape...]
    pallas_call x2, Pallas kernels: 65.2 us -> 82.1 us  [block_forward(): pl.pallas_call(functools.partial(forward_kernel, part), out_shape=[shape(...]
where the time goes in v2:
time: 404 us; the launch traced here: 397 us
  Pallas kernels  357 us (88%)
  local copies, waits for them, and re-layouts  28.6 us (7%)
  other arithmetic  8.67 us (2%)
    pallas_call x2, Pallas kernels, block_backward(): pl.pallas_call(functools.partial(backward_kernel, part), out_shape=[shape...  104 us
    pallas_call x1, Pallas kernels, reduce_grads(): pl.pallas_call(reduce_kernel, out_shape=[jax.ShapeDtypeStruct((ROWS, WIDE...  101 us
    pallas_call x2, Pallas kernels, block_forward(): pl.pallas_call(functools.partial(forward_kernel, part), out_shape=[shape(...  82.1 us
    pallas_call x1, Pallas kernels, gather_weights(): pl.pallas_call(gather_kernel, out_shape=[jax.ShapeDtypeStruct((16, ROWS,...  70 us
    unnamed x33, local copies, waits for them, and re-layouts  8.67 us

profile of v2, /device:TPU:1, one launch (start us, length us, event | category | flops | bytes accessed | tf_op | source)
XLA Modules:
  0.0 397.2 jit_solution(998194192190065836)
XLA Ops:
  0.7 0.8 reduce.1
  1.5 0.7 reduce.2
  2.2 2.1 concatenate.15
  4.9 0.7 reduce.3
  5.7 1.0 reshape_squeeze.6
  6.8 1.0 fusion.7
  7.9 0.6 broadcast_in_dim.40
  8.5 4.5 %concatenate.16.p_ref = bf16[608,768]{1,0:T(8,128)(2,1)S(1)} concatenate(bf16[144,768]{1,0:T(8,128)(2,1)S(1)} %bitcast.71, bf16[48,768]{1,0:T(8,128)(2,1)} %bitcast.87, bf16[96,768]{1,0:T(8,128)(2,1)S(1)} %bitcast.75, bf16[1,768]{1,0:T(2,128)(2,1)} %broadcast_in_dim.39, bf16[15,768]{1,0:T(8,128)(2,1)} %broadcast_in_dim.40, bf16[96,768]{1,0:T(8,128)(2,1)S(1)} %bitcast.74, ...), dimensions={0} | concatenate | bytes 1867776 | tf_op jit(solution)/shard_map/concatenate | solution.py:1028
  13.0 0.9 dynamic-slice_bitcast_fusion
  14.0 70.0 %gather_weights.1 = (bf16[16,608,768]{2,1,0:T(8,128)(2,1)S(1)}, bf16[304,768]{1,0:T(8,128)(2,1)S(1)}, f32[16,8,128]{2,1,0:T(8,128)S(1)}, f32[2,8,768]{2,1,0:T(8,128)S(1)}) custom-call(bf16[608,768]{1,0:T(8,128)(2,1)S(1)} %concatenate.16.p_ref, f32[16,8,128]{2,1,0:T(8,128)S(1)} %pad.15.conds_ref, bf16[128,4608]{1,0:T(8,128)(2,1)S(1)} %pad.16.weight_ref), custom_call_target="tpu_custom_call" | custom-call | bytes 60000000 | tf_op jit(solution)/shard_map/gather_weights/pallas_call | solution.py:341
  84.0 0.8 copy-done.5
  84.8 5.2 %copy-done.4 = bf16[16,608,768]{2,1,0:T(8,128)(2,1)} copy-done((bf16[16,608,768]{2,1,0:T(8,128)(2,1)}, bf16[16,608,768]{2,1,0:T(8,128)(2,1)S(1)}, u32[]{:S(2)}) %copy-start.4) | copy-done | bytes 14942232
  90.6 0.6 pad_maximum_fusion.1
  91.3 49.3 %forward_first.1 = (bf16[256,768]{1,0:T(8,128)(2,1)}, bf16[256,768]{1,0:T(8,128)(2,1)}, bf16[4,3,3,256,128]{4,3,2,1,0:T(8,128)(2,1)}, f32[12,1,256]{2,1,0:T(1,12...) custom-call(bf16[256,768]{1,0:T(8,128)(2,1)} %get-tuple-element.140., ...), custom_call_target="tpu_custom_call" | custom-call | flops 5000000000 | bytes 25000000 | tf_op jit(solution)/shard_map/forward_first/pallas_call | solution.py:763
  140.6 1.0 slice_convert_fusion.1
  142.0 0.6 bitcast_add_fusion.mod_ref
  142.8 0.6 pad_maximum_fusion.2.bias_ref
  143.4 32.8 %forward_second.1 = (bf16[256,768]{1,0:T(8,128)(2,1)}, bf16[256,768]{1,0:T(8,128)(2,1)}, bf16[4,3,3,256,128]{4,3,2,1,0:T(8,128)(2,1)}, f32[12,1,256]{2,1,0:T(1,1...) custom-call(bf16[256,768]{1,0:T(8,128)(2,1)} %get-tuple-element.53.x, ...), custom_call_target="tpu_custom_call" | custom-call | flops 5000000000 | bytes 25000000 | tf_op jit(solution)/shard_map/forward_second/pallas_call | solution.py:763
  176.2 45.9 %backward_second.1 = (f32[256,768]{1,0:T(8,128)}, f32[8,768]{1,0:T(8,128)}, bf16[16,608,768]{2,1,0:T(8,128)(2,1)}) custom-call(bf16[256,768]{1,0:T(8,128)(2,1)} %get-tuple-element.141.grad_ref, bf16[256,768]{1,0:T(8,128)(2,1)} %get-tuple-element.53.x_ref, f32[8,768]{1,0:T(8,128)} %bitcast_add_fusion.mod_ref, bf16[16,608,768]{2,1,0:T(8,128)(2,1)} %get-tuple-element.54.w_hbm, ...), custom_call_target="tpu_custom_call" | custom-call | flops 12000000000 | bytes 45000000 | tf_op jit(solution)/shard_map/backward_second/pallas_call | solution.py:987
  222.2 1.9 convert_element_type.41.grad_ref
  224.2 58.3 %backward_first.1 = (f32[256,768]{1,0:T(8,128)}, f32[8,768]{1,0:T(8,128)}, bf16[16,608,768]{2,1,0:T(8,128)(2,1)}, bf16[304,768]{1,0:T(8,128)(2,1)}) custom-call(bf16[256,768]{1,0:T(8,128)(2,1)} %convert_element_type.41.grad_ref, bf16[256,768]{1,0:T(8,128)(2,1)} %get-tuple-element.140.x_ref, f32[8,768]{1,0:T(8,128)} %get-tuple-element.143.mod_ref, ...), custom_call_target="tpu_custom_call" | custom-call | flops 12000000000 | bytes 45000000 | tf_op jit(solution)/shard_map/backward_first/pallas_call | solution.py:987
  282.5 1.3 convert_select_fusion
  283.8 100.9 %reduce_grads.1 = (bf16[608,768]{1,0:T(8,128)(2,1)S(1)}, f32[16,2,8,768]{3,2,1,0:T(8,128)S(1)}, f32[16,8,128]{2,1,0:T(8,128)S(1)}, bf16[2,256,768]{2,1,0:T(8,128)(2,1)S(1)}, f32[2,256,768]{2,1,0:T(8,128)}) custom-call(bf16[16,608,768]{2,1,0:T(8,128)(2,1)} %get-tuple-element.75.first_ref, bf16[304,768]{1,0:T(8,128)(2,1)S(1)} %copy-done.1, ...), custom_call_target="tpu_custom_call" | custom-call | bytes 60000000 | tf_op jit(solution)/shard_map/reduce_grads/pallas_call | solution.py:604
  386.5 0.6 dynamic_slice.27
  387.3 0.6 copy.64
  389.2 1.1 broadcast_in_dim_reshape.6
  390.2 1.2 convolution_bitcast_fusion
  391.9 1.1 broadcast_in_dim_reshape.7
  393.2 0.7 slice_bitcast_fusion.1
  393.9 0.9 slice_bitcast_fusion
  394.7 0.9 copy.89
  395.6 1.1 copy.90
  (83 shorter events, 5.9 us)
Async XLA Ops:
  0.6 13.3 %copy-start.8 = (bf16[1,48,4608]{2,1,0:T(8,128)(2,1)S(1)}, bf16[1,48,4608]{2,1,0:T(8,128)(2,1)}, u32[]{:S(2)}) copy-start(bf16[1,48,4608]{2,1,0:T(8,128)(2,1)} %param.16) | copy-start | bytes 1327108
  0.7 12.3 %copy-start.12 = (bf16[2,1,256,768]{3,2,1,0:T(8,128)(2,1)S(1)}, bf16[2,1,256,768]{3,2,1,0:T(8,128)(2,1)}, u32[]{:S(2)}) copy-start(bf16[2,1,256,768]{3,2,1,0:T(8,128)(2,1)} %param.15) | copy-start | bytes 2359300
  0.7 12.3 %copy-start.11 = (bf16[2,1,256,768]{3,2,1,0:T(8,128)(2,1)S(1)}, bf16[2,1,256,768]{3,2,1,0:T(8,128)(2,1)}, u32[]{:S(2)}) copy-start(bf16[2,1,256,768]{3,2,1,0:T(8,128)(2,1)} %param.13) | copy-start | bytes 2359300
  14.0 126.6 %copy-start = (bf16[128,4608]{1,0:T(8,128)(2,1)}, bf16[128,4608]{1,0:T(8,128)(2,1)S(1)}, u32[]{:S(2)}) copy-start(bf16[128,4608]{1,0:T(8,128)(2,1)S(1)} %pad.16.weight_ref) | copy-start | bytes 3538948
  84.0 0.8 copy-start.5
  84.7 5.3 %copy-start.4 = (bf16[16,608,768]{2,1,0:T(8,128)(2,1)}, bf16[16,608,768]{2,1,0:T(8,128)(2,1)S(1)}, u32[]{:S(2)}) copy-start(bf16[16,608,768]{2,1,0:T(8,128)(2,1)S(1)} %get-tuple-element.51.w_hbm) | copy-start | bytes 44826628
  176.2 45.9 %copy-start.9 = (bf16[256,768]{1,0:T(8,128)(2,1)S(1)}, bf16[256,768]{1,0:T(8,128)(2,1)}, u32[]{:S(2)}) copy-start(bf16[256,768]{1,0:T(8,128)(2,1)} %get-tuple-element.53.x_ref) | copy-start | bytes 1179652
  176.2 45.9 %copy-start.10 = (bf16[256,768]{1,0:T(8,128)(2,1)S(1)}, bf16[256,768]{1,0:T(8,128)(2,1)}, u32[]{:S(2)}) copy-start(bf16[256,768]{1,0:T(8,128)(2,1)} %get-tuple-element.79) | copy-start | bytes 1179652
  224.2 58.3 %copy-start.6 = (f32[256,768]{1,0:T(8,128)S(1)}, f32[256,768]{1,0:T(8,128)}, u32[]{:S(2)}) copy-start(f32[256,768]{1,0:T(8,128)} %get-tuple-element.64) | copy-start | bytes 2359300
  282.4 1.3 copy-start.1
  282.5 1.3 copy-start.2
  282.5 1.3 copy-start.3
  283.8 103.4 %copy-start.13 = (f32[2,1,768]{2,1,0:T(1,128)S(1)}, f32[2,1,768]{2,1,0:T(1,128)}, u32[]{:S(2)}) copy-start(f32[2,1,768]{2,1,0:T(1,128)} %param.14) | copy-start | bytes 18436
  393.1 2.5 copy-start.7

commit v3 on v2

--- a/solution.py
+++ b/solution.py
@@ -300,42 +300,57 @@
     return [swap[0], swap[1], multiply, add_b, add_a, end]
 
 
-def gather_kernel(p_ref, conds_ref, weight_ref, first_ref, shard_out, columns_ref, mod_ref, shard, c_first, c_second, partial, b_sums, a_sums, across_sums, local, send, recv):
+def gather_kernel(projection_ref, attention_ref, expand_ref, contract_ref, extra_ref, conds_ref, weight_ref, first_ref, shard_out, columns_ref, mod_ref, shard, c_first, c_second, partial, b_sums, a_sums, across_sums, local, send, recv):
     me = Place()
-    mine = p_ref.at[half_rows(me.c, 0, HALF), :]
-    own = pltpu.make_async_copy(mine, shard.at[me.s], local.at[2])
-    own.start()
+    columns = lambda ref, k: ref.at[:, pl.ds(k * WIDE, WIDE)]
+    halves = (
+        [columns(projection_ref, k) for k in range(3)] + [attention_ref, columns(expand_ref, 0), columns(expand_ref, 1), extra_ref],
+        [columns(expand_ref, 2), columns(expand_ref, 3), contract_ref, extra_ref],
+    )
+
+    def pack(core):
+        items, start = [], 0
+        for part in halves[core]:
+            count = part.shape[0]
+            items.append(pltpu.make_async_copy(part, shard.at[me.s, pl.ds(start, count), :], local.at[2 + len(items)]))
+            start += count
+        for item in items:
+            item.start()
+        for item in items:
+            item.wait()
+
+    for core in range(2):
+        pl.when(me.c == core)(functools.partial(pack, core))
+    mine = shard.at[me.s]
     greet(me.grid_peers() + [me.across(), me.flipped(), me.sibling()])
     wires = Wires(send, recv)
     wires.push(0, mine, shard.at[me.s], me.across())
     small = modulation_steps(me, wires, 37, conds_ref, weight_ref, columns_ref, mod_ref, c_first, c_second, partial, b_sums, a_sums, across_sums)
     small[0]()
     small[1]()
-    own.wait()
     wires.got(0, shard.at[1 - me.s], me.across())
     handed = pltpu.make_async_copy(shard.at[1], shard_out, local.at[1])
     handed.start()
     one = gather_steps(me, wires, 1, shard.at[0], first_ref, local.at[0])
     one[0]()
     small[2]()
-    one[1]()
-    one[2]()
+    for step in one[1:5]:
+        step()
     small[3]()
-    one[3]()
-    one[4]()
+    for step in one[5:8]:
+        step()
     small[4]()
-    one[5]()
-    one[6]()
+    for step in one[8:11]:
+        step()
     small[5]()
-    for step in one[7:]:
-        step()
+    one[11]()
     handed.wait()
     wires.finish()
 
 
-def gather_weights(packed, conds, weight):
+def gather_weights(*operands):
     bf, f32 = jnp.bfloat16, jnp.float32
-    wide = weight.shape[1]
+    wide = operands[-1].shape[1]
     whole = pl.BlockSpec(memory_space=pltpu.VMEM)
     away = pl.BlockSpec(memory_space=pl.ANY)
     return pl.pallas_call(
@@ -346,7 +361,7 @@
             jax.ShapeDtypeStruct((16, 8, PAIR), f32),
             jax.ShapeDtypeStruct((2, 8, WIDE), f32),
         ],
-        in_specs=[away, whole, whole],
+        in_specs=[away] * 5 + [whole, whole],
         out_specs=[away, away, whole, whole],
         scratch_shapes=[
             pltpu.VMEM((2, HALF, WIDE), bf),
@@ -356,16 +371,16 @@
             pltpu.VMEM((3, 8, wide), f32),
             pltpu.VMEM((4, 8, wide), f32),
             pltpu.VMEM((2, 8, wide), f32),
-            pltpu.SemaphoreType.DMA((3,)),
+            pltpu.SemaphoreType.DMA((9,)),
             pltpu.SemaphoreType.DMA((50,)),
             pltpu.SemaphoreType.DMA((50,)),
         ],
         compiler_params=pltpu.CompilerParams(
-            collective_id=0, has_side_effects=True, vmem_limit_bytes=24 * 1024 * 1024
+            collective_id=0, has_side_effects=True, vmem_limit_bytes=60 * 1024 * 1024
         ),
         cost_estimate=pl.CostEstimate(flops=0, bytes_accessed=60000000, transcendentals=0),
         name="gather_weights",
-    )(packed, conds, weight)
+    )(*operands)
 
 
 def reduce_steps(me, wires, base, source, load, buffers):
@@ -524,9 +539,9 @@
 
 
 def reduce_kernel(
-    first_ref, second_rows, first_terms, second_terms, weight_ref, kept_out, sent_out, kept_grad, sent_grad,
-    o_ref, all_ref, conds_ref, outs_ref, grads_ref,
-    mine, sib, r_top, r_low, r_left, r_right, a_top, a_low, a_left, a_right, final, r_across, r_beside,
+    first_ref, second_rows, first_terms, second_terms, weight_ref, kept_grad, sent_grad,
+    projection_ref, attention_ref, expand_ref, contract_ref, bias_ref, all_ref, conds_ref, grads_ref,
+    mine, sib, r_top, r_low, r_left, r_right, a_top, a_low, a_left, a_right, final, r_across, r_beside, rows, r_grad, wide_grad,
     sums, rounded, tiles, c_first, c_second, load, local, send, recv,
 ):
     me = Place()
@@ -534,48 +549,57 @@
     wires = Wires(send, recv)
     buffers = (mine, sib, r_top, r_low, r_left, r_right, a_top, a_low, a_left, a_right)
     two = reduce_steps(me, wires, 36, first_ref, load, buffers)
-    small = terms_steps(me, wires, 77, first_terms, second_terms, weight_ref, all_ref, conds_ref, sums, rounded, tiles, c_first, c_second)
+    small = terms_steps(me, wires, 86, first_terms, second_terms, weight_ref, all_ref, conds_ref, sums, rounded, tiles, c_first, c_second)
     two[0]()
     small[0]()
     keeps = [
         pltpu.make_async_copy(second_rows, final.at[1], local.at[3]),
-        pltpu.make_async_copy(kept_out, outs_ref.at[me.s], local.at[0]),
         pltpu.make_async_copy(kept_grad, grads_ref.at[me.s], local.at[1]),
     ]
     for item in keeps:
         item.start()
-    wires.push(72, sent_out, outs_ref.at[me.s], me.flipped())
-    wires.push(73, sent_grad, grads_ref.at[me.s], me.flipped())
     big = two[1:]
     small = small[1:]
     for index, step in enumerate(big):
         step()
         if index % 2 == 1 and small:
             small.pop(0)()
+        if index == 2:
+            wires.push(73, sent_grad, r_grad, me.flipped())
     while small:
         small.pop(0)()
     final[0] = mine[me.d]
     for item in keeps:
         item.wait()
+    wires.got(73, r_grad, me.flipped())
+    wide_grad[...] = r_grad[...].astype(jnp.float32)
+    came = pltpu.make_async_copy(wide_grad, grads_ref.at[1 - me.s], local.at[0])
+    came.start()
     held = final.at[me.s]
-    wires.push(74, final.at[1 - me.s], r_across, me.across())
-    wires.got(74, r_across, me.across())
-    add_rows(held, [(r_across, 0)])
-    beside = pltpu.make_async_remote_copy(
-        src_ref=held, dst_ref=r_beside, send_sem=send.at[75], recv_sem=recv.at[75], device_id=me.beside(), device_id_type=MESH
-    )
-    beside.start()
-    wires.got(75, r_beside, me.beside())
-    beside.wait_send()
-    add_rows(held, [(r_beside, 0)])
-    out_rows = o_ref.at[half_rows(me.c, 0, HALF), :]
-    wires.push(76, held, out_rows, me.sibling())
-    own = pltpu.make_async_copy(held, out_rows, local.at[2])
-    own.start()
-    own.wait()
-    wires.got(72, outs_ref.at[1 - me.s], me.flipped())
-    wires.got(73, grads_ref.at[1 - me.s], me.flipped())
-    wires.got(76, o_ref.at[half_rows(1 - me.c, 0, HALF), :], me.sibling())
+    cuts = ((0, 80), (80, 80), (160, 80), (240, 64))
+    for n, (start, count) in enumerate(cuts):
+        part = pl.ds(start, count)
+        wires.push(74 + n, final.at[1 - me.s, part, :], r_across.at[part, :], me.across())
+    for n, (start, count) in enumerate(cuts):
+        part = pl.ds(start, count)
+        wires.got(74 + n, r_across.at[part, :], me.across())
+        add_rows(held, [(r_across, 0)], start, count)
+        wires.push(78 + n, held.at[part, :], r_beside.at[part, :], me.beside())
+    for n, (start, count) in enumerate(cuts):
+        part = pl.ds(start, count)
+        wires.got(78 + n, r_beside.at[part, :], me.beside())
+        total = held[part, :].astype(jnp.float32) + r_beside[part, :].astype(jnp.float32)
+        rows[half_rows(me.c, start, count), :] = total.astype(jnp.bfloat16)
+        block = rows.at[half_rows(me.c, start, count), :]
+        wires.push(82 + n, block, block, me.sibling())
+    for n, (start, count) in enumerate(cuts):
+        wires.got(82 + n, rows.at[half_rows(1 - me.c, start, count), :], me.sibling())
+    for ref, starts in ((projection_ref, (0, 48, 96)), (attention_ref, (144,)), (expand_ref, EXPAND_ROWS)):
+        for k, start in enumerate(starts):
+            ref[:, k * WIDE : (k + 1) * WIDE] = rows[start : start + 48, :].astype(jnp.float32)
+    contract_ref[...] = rows[CONTRACT_ROW : CONTRACT_ROW + 192, :].astype(jnp.float32)
+    bias_ref[...] = rows[BIAS_ROW : BIAS_ROW + 16, :].astype(jnp.float32)
+    came.wait()
     wires.finish()
 
 
@@ -596,7 +620,7 @@
 
 
 def reduce_grads(*operands):
-    count = 77 + 26
+    count = 86 + 26
     bf, f32 = jnp.bfloat16, jnp.float32
     blocks = lambda *lead: pltpu.VMEM(lead + (WIDE,), bf)
     whole = pl.BlockSpec(memory_space=pltpu.VMEM)
@@ -604,19 +628,25 @@
     return pl.pallas_call(
         reduce_kernel,
         out_shape=[
-            jax.ShapeDtypeStruct((ROWS, WIDE), bf),
+            jax.ShapeDtypeStruct((48, 3 * WIDE), f32),
+            jax.ShapeDtypeStruct((48, WIDE), f32),
+            jax.ShapeDtypeStruct((48, 4 * WIDE), f32),
+            jax.ShapeDtypeStruct((192, WIDE), f32),
+            jax.ShapeDtypeStruct((16, WIDE), f32),
             jax.ShapeDtypeStruct((16, 2, 8, WIDE), f32),
             jax.ShapeDtypeStruct((16, 8, PAIR), f32),
-            jax.ShapeDtypeStruct((2, TOKENS, WIDE), bf),
             jax.ShapeDtypeStruct((2, TOKENS, WIDE), f32),
         ],
-        in_specs=[away, away, whole, whole, whole, away, away, away, away],
-        out_specs=[away, whole, whole, away, away],
+        in_specs=[away, away, whole, whole, whole, away, away],
+        out_specs=[whole] * 7 + [away],
         scratch_shapes=[
             *reduce_buffers(),
             blocks(2, HALF),
             blocks(HALF),
             blocks(HALF),
+            blocks(ROWS),
+            blocks(TOKENS),
+            pltpu.VMEM((TOKENS, WIDE), f32),
             pltpu.VMEM((4, 2, 8, WIDE), f32),
             pltpu.VMEM((2, 8, WIDE), f32),
             pltpu.VMEM((3, 16, 8, PAIR), f32),
@@ -709,8 +739,8 @@
                 powers = jnp.exp(scores - top)
                 sums = jnp.sum(powers, axis=0, keepdims=True)
                 lse_ref[(2 * j + head) * 2 + g] = top + jnp.log(sums)
-                weights = (powers * (1.0 / sums)).astype(jnp.bfloat16)
-                made.append(dot(values, weights, 0, 0)[head * HEAD : (head + 1) * HEAD])
+                weights = powers.astype(jnp.bfloat16)
+                made.append(dot(values, weights, 0, 0)[head * HEAD : (head + 1) * HEAD] * (1.0 / sums))
             heads[g, j] = jnp.concatenate(made, axis=0).T.astype(jnp.bfloat16)
             return carry
 
@@ -800,9 +830,13 @@
 def backward_kernel(
     part, grad_ref, x_ref, mod_ref, w_hbm, mixed_one_ref, qkv_in, lse_ref, att_ref, branch_one_ref, middle_ref, mixed_two_ref, expanded_in, branch_two_ref, *refs
 ):
-    later_ref, refs = (refs[0], refs[1:]) if part == 0 else (None, refs)
+    if part == 0:
+        later_ref, *refs = refs
+    else:
+        kept_out, sent_out, *refs = refs
     input_grad_ref, terms_ref, grads_out, *refs = refs
-    rows_out, refs = (refs[0], refs[1:]) if part == 0 else (None, refs)
+    extra_out, *refs = refs
+    carried, refs = (input_grad_ref, refs) if part == 0 else (refs[0], refs[1:])
     w, expanded, qkv, stage, given, dkv, dq, own, far_out, far_in, side_out, side_in, joined, load, save, send, recv, *refs = refs
     me = Place()
     sibling, far = seq_peers(me)
@@ -815,7 +849,7 @@
     expanded_load.start()
     front_load.start()
     qkv_load.start()
-    around = [me.ring(1, 0), me.ring(3, 0), me.ring(0, 1), me.ring(0, 3)] if part == 0 else []
+    around = [me.ring(1, 0), me.ring(3, 0), me.ring(0, 1), me.ring(0, 3)] if part == 0 else [me.flipped()]
     greet([sibling, *far, *around])
     wires = Wires(send, recv)
     beside = reduce_steps(me, wires, 10, later_ref, refs[-1], refs[:-1]) if part == 0 else []
@@ -825,6 +859,10 @@
             beside.pop(0)()
 
     advance(1)
+    if part == 1:
+        keep_out = pltpu.make_async_copy(kept_out, extra_out.at[me.s], load.at[4])
+        keep_out.start()
+        wires.push(10, sent_out, extra_out.at[me.s], me.flipped())
     saves = []
 
     def keep(index, start, count):
@@ -875,7 +913,7 @@
     wires.push(0, stage.at[pl.ds(3 * other, 3)], given.at[c], sibling)
     advance(1)
     given[c] = stage[pl.ds(3 * c, 3)]
-    input_grad_ref[...] = middle_grad
+    carried[...] = middle_grad
     w[:, 144:192, :] = dot(side_by_side(att_ref), branch_one_grad, 0, 0).astype(jnp.bfloat16).reshape(16, 48, WIDE)
     keep(2, 144, 48)
     attention_bias_grad = column_sum(branch_one_grad)
@@ -968,12 +1006,16 @@
         ],
         axis=0,
     )
-    input_grad_ref[...] += norm_back(mixed_one_grad * (1.0 + row(1)), normed_one, inv_one)
+    result = carried[...] + norm_back(mixed_one_grad * (1.0 + row(1)), normed_one, inv_one)
+    input_grad_ref[...] = result.astype(input_grad_ref.dtype)
     advance(16)
     if part == 0:
-        rows_save = pltpu.make_async_copy(refs[0].at[me.d], rows_out, load.at[0])
+        rows_save = pltpu.make_async_copy(refs[0].at[me.d], extra_out, load.at[0])
         rows_save.start()
         rows_save.wait()
+    else:
+        keep_out.wait()
+        wires.got(10, extra_out.at[1 - me.s], me.flipped())
     for item in saves:
         item.wait()
     wires.finish()
@@ -987,14 +1029,15 @@
     return pl.pallas_call(
         functools.partial(backward_kernel, part),
         out_shape=[
-            shape((TOKENS, WIDE), f32),
+            shape((TOKENS, WIDE), f32 if part == 0 else bf),
             shape((8, WIDE), f32),
             shape((16, ROWS, WIDE), bf),
         ]
-        + [shape((HALF, WIDE), bf) for _ in later],
+        + [shape((HALF, WIDE), bf) if part == 0 else shape((2, TOKENS, WIDE), bf)],
         in_specs=[whole, whole, whole, away, whole, away, whole, whole, whole, whole, whole, away, whole] + [away for _ in later],
-        out_specs=[whole, whole, away] + [away for _ in later],
-        scratch_shapes=[
+        out_specs=[whole, whole, away, away],
+        scratch_shapes=([] if part == 0 else [pltpu.VMEM((TOKENS, WIDE), f32)])
+        + [
             pltpu.VMEM((16, ROWS, WIDE), bf),
             pltpu.VMEM((4, TOKENS, WIDE), f32),
             pltpu.VMEM((4, 3, 3, TOKENS, PAIR), bf),
@@ -1008,35 +1051,18 @@
             pltpu.VMEM((3, 3, TOKENS, PAIR), bf),
             pltpu.VMEM((3, 3, TOKENS, PAIR), bf),
             pltpu.VMEM((3, 6, TOKENS, PAIR), bf),
-            pltpu.SemaphoreType.DMA((4,)),
+            pltpu.SemaphoreType.DMA((5,)),
             pltpu.SemaphoreType.DMA((6,)),
             pltpu.SemaphoreType.DMA((46,)),
             pltpu.SemaphoreType.DMA((46,)),
         ]
-        + ([*reduce_buffers(), pltpu.SemaphoreType.DMA((16,))] if later else []),
+        + ([*reduce_buffers(), pltpu.SemaphoreType.DMA((16,))] if part == 0 else []),
         compiler_params=pltpu.CompilerParams(
             collective_id=4 + part, has_side_effects=True, vmem_limit_bytes=60 * 1024 * 1024
         ),
         cost_estimate=pl.CostEstimate(flops=12 * 10**9, bytes_accessed=45 * 10**6, transcendentals=4 * 10**6),
         name=("backward_first", "backward_second")[part],
     )(gradient, tokens, modulation, blocks, *kept, *later)
-
-
-def pack_weights(projection, attention, expand, contract, biases):
-    fill = jnp.zeros((WIDE - biases.shape[0],), jnp.bfloat16)
-    columns = lambda weight: weight.reshape(48, -1, WIDE).swapaxes(0, 1).reshape(-1, WIDE)
-    return jnp.concatenate(
-        [
-            columns(projection),
-            attention,
-            columns(expand[:, : 2 * WIDE]),
-            jnp.concatenate([biases, fill])[None],
-            jnp.zeros((15, WIDE), jnp.bfloat16),
-            columns(expand[:, 2 * WIDE :]),
-            contract,
-            jnp.zeros((16, WIDE), jnp.bfloat16),
-        ]
-    )
 
 
 def bias_rows(biases):
@@ -1050,18 +1076,17 @@
     return jnp.concatenate(parts), added
 
 
-def unpack_grads(rows, place):
-    columns = lambda part: part.reshape(-1, 48, WIDE).swapaxes(0, 1).reshape(48, -1)
+def with_biases(made, bias, place):
     own = lambda part, size: lax.dynamic_slice_in_dim(part.reshape(-1), place * size, size)
-    bias = rows[BIAS_ROW : BIAS_ROW + 8]
+    projection, attention, expand, contract = made
     return [
-        columns(rows[:144]),
+        projection,
         own(bias[0:2], 96),
-        rows[144:192],
+        attention,
         own(bias[2:3], 48),
-        columns(jnp.concatenate([rows[192:288], rows[304:400]])),
+        expand,
         own(bias[3:7], 192),
-        rows[400:592],
+        contract,
         own(bias[7:8], 48),
     ]
 
@@ -1087,10 +1112,12 @@
     biases = jnp.concatenate(
         [projection_bias[0], attention_bias[0], expand_bias[0], contract_bias[0], modulation_bias[0]]
     )
-    packed = pack_weights(projection_weight[0], attention_weight[0], expand_weight[0], contract_weight[0], biases)
+    extra = jnp.pad(biases[None], ((0, 15), (0, WIDE - biases.shape[0])))
     pieces = jnp.pad(conditions[:, 0].reshape(2, 16, 48).swapaxes(0, 1), ((0, 0), (0, 6), (0, PAIR - 48)))
     owned_weight = jnp.pad(modulation_weight[0], ((0, PAIR - 48), (0, 0)))
-    first_blocks, shard, own_conds, modulations = gather_weights(packed, pieces, owned_weight)
+    first_blocks, shard, own_conds, modulations = gather_weights(
+        projection_weight[0], attention_weight[0], expand_weight[0], contract_weight[0], extra, pieces, owned_weight
+    )
     first_bias, first_added = bias_rows(first_blocks[:, BIAS_ROW].astype(jnp.float32))
     first_modulation = modulations[0] + first_added
 
@@ -1100,27 +1127,31 @@
     second_bias, second_added = bias_rows(second_blocks[:, BIAS_ROW].astype(jnp.float32))
     second_modulation = modulations[1] + second_added
     second_output, *second_kept = block_forward(1, first_output, second_modulation, second_bias, second_blocks)
-    second_grad, second_terms, second_made = block_backward(
-        1, cotangent, first_output, second_modulation, second_blocks, second_kept
+    second_grad, second_terms, second_made, section_outputs = block_backward(
+        1,
+        cotangent,
+        first_output,
+        second_modulation,
+        second_blocks,
+        second_kept,
+        jnp.where(is_first, first_output, second_output),
+        jnp.where(is_first, second_output, first_output),
     )
-    second_grad = second_grad.astype(jnp.bfloat16)
     first_grad, first_terms, first_made, second_rows = block_backward(
         0, second_grad, tokens, first_modulation, first_blocks, first_kept, second_made
     )
 
     rounded_grad = second_grad.astype(jnp.float32)
-    rows, terms, cond_terms, section_outputs, input_grads = reduce_grads(
+    *made, bias, terms, cond_terms, input_grads = reduce_grads(
         first_made,
         second_rows,
         first_terms,
         second_terms,
         owned_weight,
-        jnp.where(is_first, first_output, second_output),
-        jnp.where(is_first, second_output, first_output),
         jnp.where(is_first, first_grad, rounded_grad),
-        jnp.where(is_first, rounded_grad, first_grad),
+        jnp.where(is_first, second_grad, first_grad.astype(jnp.bfloat16)),
     )
-    reduced = [grad[None] for grad in unpack_grads(rows.astype(jnp.float32), place)]
+    reduced = [grad[None] for grad in with_biases(made, bias, place)]
     section_outputs = section_outputs[None, :, None]
     input_grads = input_grads[None, :, None]
     terms = terms[:, :, :6].reshape(16, 2, -1)

time: 404 us -> 369 us (0.913)
  Pallas kernels: 357 us -> 331 us
  local copies, waits for them, and re-layouts: 28.6 us -> 19 us
    pallas_call x1, Pallas kernels: 101 us -> 72.6 us  [reduce_grads(): pl.pallas_call(reduce_kernel, out_shape=[jax.ShapeDtypeStruct((48, 3 * WI...]
    concatenate x2 -> x1, local copies, waits for them, and re-layouts: 6.54 us -> 2.09 us  [on_device(): jnp.concatenate([projection_bias[0], attention_bias[0], expand_bias[0], c...]
    unnamed x33 -> x27, local copies, waits for them, and re-layouts: 8.67 us -> 6.91 us
where the time goes in v3:
time: 369 us; the launch traced here: 364 us
  Pallas kernels  331 us (90%)
  local copies, waits for them, and re-layouts  19 us (5%)
  other arithmetic  12 us (3%)
    pallas_call x2, Pallas kernels, block_backward(): pl.pallas_call(functools.partial(backward_kernel, part), out_shape=[shape...  104 us
    pallas_call x2, Pallas kernels, block_forward(): pl.pallas_call(functools.partial(forward_kernel, part), out_shape=[shape(...  81.6 us
    pallas_call x1, Pallas kernels, gather_weights(): pl.pallas_call(gather_kernel, out_shape=[jax.ShapeDtypeStruct((16, ROWS,...  72.7 us
    pallas_call x1, Pallas kernels, reduce_grads(): pl.pallas_call(reduce_kernel, out_shape=[jax.ShapeDtypeStruct((48, 3 * WI...  72.6 us

profile of v3, /device:TPU:1, one launch (start us, length us, event | category | flops | bytes accessed | tf_op | source)
XLA Modules:
  0.0 364.3 jit_solution(223775446145274057)
XLA Ops:
  0.7 0.7 reduce.1
  1.4 0.7 reduce.2
  2.1 2.1 concatenate.9
  4.1 0.7 reduce.3
  5.0 0.6 pad.19.extra_ref
  5.6 0.6 pad.20.conds_ref
  6.2 2.0 dynamic-slice_bitcast_fusion
  8.3 2.1 pad.21.weight_ref
  10.4 72.7 %gather_weights.1 = (bf16[16,608,768]{2,1,0:T(8,128)(2,1)}, bf16[304,768]{1,0:T(8,128)(2,1)}, f32[16,8,128]{2,1,0:T(8,128)}, f32[2,8,768]{2,1,0:T(8,128)}) custom-call(bf16[48,2304]{1,0:T(8,128)(2,1)} %bitcast.60, bf16[48,768]{1,0:T(8,128)(2,1)} %bitcast.61, bf16[48,3072]{1,0:T(8,128)(2,1)} %bitcast.50, bf16[192,768]{1,0:T(8,128)(2,1)} %bitcast.51, ...), custom_call_target="tpu_custom_call" | custom-call | bytes 60000000 | tf_op jit(solution)/shard_map/gather_weights/pallas_call | solution.py:356
  83.1 0.9 fusion.1
  84.0 1.0 slice_convert_fusion.2
  85.5 1.4 pad_maximum_fusion
  86.9 49.2 %forward_first.1 = (bf16[256,768]{1,0:T(8,128)(2,1)}, bf16[256,768]{1,0:T(8,128)(2,1)}, bf16[4,3,3,256,128]{4,3,2,1,0:T(8,128)(2,1)}, f32[12,1,256]{2,1,0:T(1,12...) custom-call(bf16[256,768]{1,0:T(8,128)(2,1)} %get-tuple-element.142., ...), custom_call_target="tpu_custom_call" | custom-call | flops 5000000000 | bytes 25000000 | tf_op jit(solution)/shard_map/forward_first/pallas_call | solution.py:793
  136.1 1.0 slice_convert_fusion.1
  137.5 0.6 bitcast_add_fusion.mod_ref
  138.3 0.6 pad_maximum_fusion.1.bias_ref
  138.9 32.3 %forward_second.1 = (bf16[256,768]{1,0:T(8,128)(2,1)}, bf16[256,768]{1,0:T(8,128)(2,1)}, bf16[4,3,3,256,128]{4,3,2,1,0:T(8,128)(2,1)}, f32[12,1,256]{2,1,0:T(1,1...) custom-call(bf16[256,768]{1,0:T(8,128)(2,1)} %get-tuple-element.57.x, ...), custom_call_target="tpu_custom_call" | custom-call | flops 5000000000 | bytes 25000000 | tf_op jit(solution)/shard_map/forward_second/pallas_call | solution.py:793
  171.3 1.9 broadcast_select_fusion
  173.2 45.8 %backward_second.1 = (bf16[256,768]{1,0:T(8,128)(2,1)}, f32[8,768]{1,0:T(8,128)}, bf16[16,608,768]{2,1,0:T(8,128)(2,1)}, bf16[2,256,768]{2,1,0:T(8,128)(2,1)}) custom-call(bf16[256,768]{1,0:T(8,128)(2,1)} %get-tuple-element.143.grad_ref, bf16[256,768]{1,0:T(8,128)(2,1)} %get-tuple-element.57.x_ref, f32[8,768]{1,0:T(8,128)} %bitcast_add_fusion.mod_ref, ...), custom_call_target="tpu_custom_call" | custom-call | flops 12000000000 | bytes 45000000 | tf_op jit(solution)/shard_map/backward_second/pallas_call | solution.py:1029
  219.0 58.2 %backward_first.1 = (f32[256,768]{1,0:T(8,128)}, f32[8,768]{1,0:T(8,128)}, bf16[16,608,768]{2,1,0:T(8,128)(2,1)}, bf16[304,768]{1,0:T(8,128)(2,1)}) custom-call(bf16[256,768]{1,0:T(8,128)(2,1)} %get-tuple-element.70.grad_ref, bf16[256,768]{1,0:T(8,128)(2,1)} %get-tuple-element.142.x_ref, f32[8,768]{1,0:T(8,128)} %get-tuple-element.145.mod_ref, ...), custom_call_target="tpu_custom_call" | custom-call | flops 12000000000 | bytes 45000000 | tf_op jit(solution)/shard_map/backward_first/pallas_call | solution.py:1029
  277.3 1.3 convert_select_fusion.1.sent_grad
  278.6 1.2 convert_select_fusion.kept_grad
  279.9 72.6 %reduce_grads.1 = (f32[48,2304]{1,0:T(8,128)S(1)}, f32[48,768]{1,0:T(8,128)S(1)}, f32[48,3072]{1,0:T(8,128)S(1)}, f32[192,768]{1,0:T(8,128)S(1)}, f32[16,768]{1,...) custom-call(bf16[16,608,768]{2,1,0:T(8,128)(2,1)} %get-tuple-element.81.first_ref, ...), custom_call_target="tpu_custom_call" | custom-call | bytes 60000000 | tf_op jit(solution)/shard_map/reduce_grads/pallas_call | solution.py:628
  353.1 0.6 dynamic_slice.27
  355.1 0.6 copy.49
  356.6 1.2 convolution_bitcast_fusion
  357.9 2.1 copy.70
  359.9 1.1 copy.71
  361.1 0.8 copy.72
  361.8 0.7 copy.73
  362.5 0.8 copy.74
  363.3 0.8 copy.75
  (59 shorter events, 4.1 us)
Async XLA Ops:
  86.9 50.6 %copy-start.7 = (f32[2,8,768]{2,1,0:T(8,128)S(1)}, f32[2,8,768]{2,1,0:T(8,128)}, u32[]{:S(2)}) copy-start(f32[2,8,768]{2,1,0:T(8,128)} %get-tuple-element.54) | copy-start | bytes 147460
  138.9 32.3 %copy-start.6 = (bf16[256,768]{1,0:T(8,128)(2,1)S(1)}, bf16[256,768]{1,0:T(8,128)(2,1)}, u32[]{:S(2)}) copy-start(bf16[256,768]{1,0:T(8,128)(2,1)} %get-tuple-element.57.x_ref) | copy-start | bytes 1179652
  219.0 58.3 %copy-start.5 = (bf16[256,768]{1,0:T(8,128)(2,1)S(1)}, bf16[256,768]{1,0:T(8,128)(2,1)}, u32[]{:S(2)}) copy-start(bf16[256,768]{1,0:T(8,128)(2,1)} %get-tuple-element.70.grad_ref) | copy-start | bytes 1179652
  277.2 2.6 copy-start
  277.2 2.6 copy-start.1
  277.3 2.6 copy-start.2
  277.3 2.6 copy-start.3
  279.8 75.2 %copy-start.8 = (f32[2,1,768]{2,1,0:T(1,128)S(1)}, f32[2,1,768]{2,1,0:T(1,128)}, u32[]{:S(2)}) copy-start(f32[2,1,768]{2,1,0:T(1,128)} %param.14) | copy-start | bytes 18436
  356.0 3.9 %copy-start.4 = (f32[2,256,768]{2,1,0:T(8,128)S(1)}, f32[2,256,768]{2,1,0:T(8,128)}, u32[]{:S(2)}) copy-start(f32[2,256,768]{2,1,0:T(8,128)} %get-tuple-element.86) | copy-start | bytes 4718596

commit v4 on v3

--- a/solution.py
+++ b/solution.py
@@ -481,7 +481,7 @@
         target[rows, :] = value.astype(jnp.bfloat16)
         return carry
 
-    lax.fori_loop(0, count // 16, step, 0)
+    lax.fori_loop(0, count // 16, step, 0, unroll=True)
 
 
 def terms_steps(me, wires, base, first_ref, second_ref, weight_ref, all_ref, conds_ref, sums, rounded, tiles, c_first, c_second):

time: 369 us -> 367 us (level)
  no operation moved by 1% of the time
where the time goes in v4:
time: 367 us; the launch traced here: 363 us
  Pallas kernels  330 us (90%)
  local copies, waits for them, and re-layouts  19 us (5%)
  other arithmetic  12 us (3%)
    pallas_call x2, Pallas kernels, block_backward(): pl.pallas_call(functools.partial(backward_kernel, part), out_shape=[shape...  103 us
    pallas_call x2, Pallas kernels, block_forward(): pl.pallas_call(functools.partial(forward_kernel, part), out_shape=[shape(...  81.9 us
    pallas_call x1, Pallas kernels, gather_weights(): pl.pallas_call(gather_kernel, out_shape=[jax.ShapeDtypeStruct((16, ROWS,...  72.7 us
    pallas_call x1, Pallas kernels, reduce_grads(): pl.pallas_call(reduce_kernel, out_shape=[jax.ShapeDtypeStruct((48, 3 * WI...  72.2 us

profile of v4, /device:TPU:1, one launch (start us, length us, event | category | flops | bytes accessed | tf_op | source)
XLA Modules:
  0.0 363.0 jit_solution(4018740587197688841)
XLA Ops:
  0.7 0.7 reduce.1
  1.4 0.7 reduce.2
  2.1 2.1 concatenate.9
  4.1 0.7 reduce.3
  5.0 0.6 pad.19.extra_ref
  5.6 0.6 pad.20.conds_ref
  6.2 2.0 dynamic-slice_bitcast_fusion
  8.3 2.1 pad.21.weight_ref
  10.4 72.7 %gather_weights.1 = (bf16[16,608,768]{2,1,0:T(8,128)(2,1)}, bf16[304,768]{1,0:T(8,128)(2,1)}, f32[16,8,128]{2,1,0:T(8,128)}, f32[2,8,768]{2,1,0:T(8,128)}) custom-call(bf16[48,2304]{1,0:T(8,128)(2,1)} %bitcast.60, bf16[48,768]{1,0:T(8,128)(2,1)} %bitcast.61, bf16[48,3072]{1,0:T(8,128)(2,1)} %bitcast.50, bf16[192,768]{1,0:T(8,128)(2,1)} %bitcast.51, ...), custom_call_target="tpu_custom_call" | custom-call | bytes 60000000 | tf_op jit(solution)/shard_map/gather_weights/pallas_call | solution.py:356
  83.1 0.9 fusion.1
  84.0 1.0 slice_convert_fusion.2
  85.5 1.4 pad_maximum_fusion
  86.9 49.2 %forward_first.1 = (bf16[256,768]{1,0:T(8,128)(2,1)}, bf16[256,768]{1,0:T(8,128)(2,1)}, bf16[4,3,3,256,128]{4,3,2,1,0:T(8,128)(2,1)}, f32[12,1,256]{2,1,0:T(1,12...) custom-call(bf16[256,768]{1,0:T(8,128)(2,1)} %get-tuple-element.142., ...), custom_call_target="tpu_custom_call" | custom-call | flops 5000000000 | bytes 25000000 | tf_op jit(solution)/shard_map/forward_first/pallas_call | solution.py:793
  136.1 1.0 slice_convert_fusion.1
  137.5 0.6 bitcast_add_fusion.mod_ref
  138.3 0.6 pad_maximum_fusion.1.bias_ref
  138.9 32.6 %forward_second.1 = (bf16[256,768]{1,0:T(8,128)(2,1)}, bf16[256,768]{1,0:T(8,128)(2,1)}, bf16[4,3,3,256,128]{4,3,2,1,0:T(8,128)(2,1)}, f32[12,1,256]{2,1,0:T(1,1...) custom-call(bf16[256,768]{1,0:T(8,128)(2,1)} %get-tuple-element.57.x, ...), custom_call_target="tpu_custom_call" | custom-call | flops 5000000000 | bytes 25000000 | tf_op jit(solution)/shard_map/forward_second/pallas_call | solution.py:793
  171.6 1.9 broadcast_select_fusion
  173.5 45.6 %backward_second.1 = (bf16[256,768]{1,0:T(8,128)(2,1)}, f32[8,768]{1,0:T(8,128)}, bf16[16,608,768]{2,1,0:T(8,128)(2,1)}, bf16[2,256,768]{2,1,0:T(8,128)(2,1)}) custom-call(bf16[256,768]{1,0:T(8,128)(2,1)} %get-tuple-element.143.grad_ref, bf16[256,768]{1,0:T(8,128)(2,1)} %get-tuple-element.57.x_ref, f32[8,768]{1,0:T(8,128)} %bitcast_add_fusion.mod_ref, ...), custom_call_target="tpu_custom_call" | custom-call | flops 12000000000 | bytes 45000000 | tf_op jit(solution)/shard_map/backward_second/pallas_call | solution.py:1029
  219.1 57.2 %backward_first.1 = (f32[256,768]{1,0:T(8,128)}, f32[8,768]{1,0:T(8,128)}, bf16[16,608,768]{2,1,0:T(8,128)(2,1)}, bf16[304,768]{1,0:T(8,128)(2,1)}) custom-call(bf16[256,768]{1,0:T(8,128)(2,1)} %get-tuple-element.70.grad_ref, bf16[256,768]{1,0:T(8,128)(2,1)} %get-tuple-element.142.x_ref, f32[8,768]{1,0:T(8,128)} %get-tuple-element.145.mod_ref, ...), custom_call_target="tpu_custom_call" | custom-call | flops 12000000000 | bytes 45000000 | tf_op jit(solution)/shard_map/backward_first/pallas_call | solution.py:1029
  276.4 1.3 convert_select_fusion.1.sent_grad
  277.7 1.2 convert_select_fusion.kept_grad
  279.0 72.2 %reduce_grads.1 = (f32[48,2304]{1,0:T(8,128)S(1)}, f32[48,768]{1,0:T(8,128)S(1)}, f32[48,3072]{1,0:T(8,128)S(1)}, f32[192,768]{1,0:T(8,128)S(1)}, f32[16,768]{1,...) custom-call(bf16[16,608,768]{2,1,0:T(8,128)(2,1)} %get-tuple-element.81.first_ref, ...), custom_call_target="tpu_custom_call" | custom-call | bytes 60000000 | tf_op jit(solution)/shard_map/reduce_grads/pallas_call | solution.py:628
  351.8 0.6 dynamic_slice.27
  353.8 0.6 copy.49
  355.3 1.2 convolution_bitcast_fusion
  356.6 2.1 copy.70
  358.6 1.1 copy.71
  359.8 0.8 copy.72
  360.5 0.7 copy.73
  361.2 0.8 copy.74
  362.0 0.8 copy.75
  (59 shorter events, 4.1 us)
Async XLA Ops:
  86.9 50.6 %copy-start.7 = (f32[2,8,768]{2,1,0:T(8,128)S(1)}, f32[2,8,768]{2,1,0:T(8,128)}, u32[]{:S(2)}) copy-start(f32[2,8,768]{2,1,0:T(8,128)} %get-tuple-element.54) | copy-start | bytes 147460
  138.9 32.7 %copy-start.6 = (bf16[256,768]{1,0:T(8,128)(2,1)S(1)}, bf16[256,768]{1,0:T(8,128)(2,1)}, u32[]{:S(2)}) copy-start(bf16[256,768]{1,0:T(8,128)(2,1)} %get-tuple-element.57.x_ref) | copy-start | bytes 1179652
  219.1 57.3 %copy-start.5 = (bf16[256,768]{1,0:T(8,128)(2,1)S(1)}, bf16[256,768]{1,0:T(8,128)(2,1)}, u32[]{:S(2)}) copy-start(bf16[256,768]{1,0:T(8,128)(2,1)} %get-tuple-element.70.grad_ref) | copy-start | bytes 1179652
  276.4 2.6 copy-start
  276.4 2.6 copy-start.1
  276.4 2.6 copy-start.2
  276.4 2.6 copy-start.3
  279.0 74.8 %copy-start.8 = (f32[2,1,768]{2,1,0:T(1,128)S(1)}, f32[2,1,768]{2,1,0:T(1,128)}, u32[]{:S(2)}) copy-start(f32[2,1,768]{2,1,0:T(1,128)} %param.14) | copy-start | bytes 18436
  354.7 3.9 %copy-start.4 = (f32[2,256,768]{2,1,0:T(8,128)S(1)}, f32[2,256,768]{2,1,0:T(8,128)}, u32[]{:S(2)}) copy-start(f32[2,256,768]{2,1,0:T(8,128)} %get-tuple-element.86) | copy-start | bytes 4718596
